TPU v7x, 512 devices: a whole 4x4x16 slice. The times are simulated.
512 devices in a mesh: rows: 128 (over x, z, core), cells: 4 (over y).
Axes of the slice: x: 4, y: 4, z: 16, core: 2. Of those that a mesh axis runs over, the one named last changes fastest.
Arguments:
- row_profile: bfloat16 [4, 2097152], P(None, ('rows', 'cells')), may hold values from 0.029907227 to 0.29882812
- col_profile: bfloat16 [16, 2097152], P(None, ('rows', 'cells')), may hold values from 0.029907227 to 0.29882812
- send_list: int32 [262144, 16], P(('rows', 'cells')), may hold values from 0 to 4096, as said below
- tile_list: int32 [16384, 256], P(('rows', 'cells')), may hold values from 0 to 8192, as said below
- row_offset: int32 [16384, 256], P(('rows', 'cells')), may hold values from 0 to 4
- col_offset: int32 [16384, 256], P(('rows', 'cells')), may hold values from 0 to 112
- macro_mask: int32 [4096, 4096], P(('rows', 'cells')), may hold values 0 or 1
Outputs:
- fields: bfloat16 [2, 4096, 4096], P(None, ('rows', 'cells'))
- force: float32 [2, 2097152], P(None, ('rows', 'cells'))
Inputs may be any that keep to these rules, and one draw needn't show every extreme that they name: `send_list`: in row s * 512 + d the filled slots come first and hold distinct cells of block s; every cell of a block is listed exactly once over its 512 rows; 4096 marks an empty slot; every cell block fills all 16 slots of some rows. `tile_list`: each bin block receives exactly 4096 filled slots, and each of them is listed exactly once over that block's 32 tiles; filled places come first in a row; 8192 marks an empty place; every bin block has tiles with all 256 places filled.
All inputs are finite; a program needn't handle non-finite values. No bound on the sum of `macro_mask` on one device may be relied on, other than what follows from the above.
Results may differ from a plain program's by a relative error of at most 0.0017.
Values may be sent and summed in bfloat16 or wider, within the bound.
No kernel may reach another device: no remote copies, remote signals or barrier semaphores. Data moves between devices by JAX's collectives and lax.ppermute only.
A program may use at most 64 MiB of HBM per device.

v0:
```python
import math

import jax
import jax.numpy as jnp
from jax import lax
from jax.sharding import PartitionSpec as P

TW = 128
BH = 4
BW = 16


HIGHEST = lax.Precision.HIGHEST
MACRO_LEVEL = 4.0


def section_table(count_rows, count_cols, period, direction):
    first_index = lax.broadcasted_iota(jnp.int32, (count_rows, count_cols), 0)
    second_index = lax.broadcasted_iota(jnp.int32, (count_rows, count_cols), 1)
    turned = (first_index * second_index % period).astype(jnp.float32) * (2.0 * math.pi / period)
    return (jnp.cos(turned), direction * jnp.sin(turned))


def half_transform(real_part, imag_part, direction, batch_last):
    extent = real_part.shape[0] if batch_last else real_part.shape[1]
    batch_count = real_part.shape[1] if batch_last else real_part.shape[0]
    padded = 2 * extent
    outer_size = 1 << (padded.bit_length() - 1) // 2
    inner_size = padded // outer_size
    if batch_last:
        spec_one = "pqb,np->bnq"
        shape_in = (outer_size // 2, inner_size, batch_count)
    else:
        spec_one = "bpq,np->bnq"
        shape_in = (batch_count, outer_size // 2, inner_size)
    cos_one, sin_one = section_table(outer_size, outer_size // 2, outer_size, direction)
    real_in = real_part.reshape(shape_in)
    acc_real = jnp.einsum(spec_one, real_in, cos_one, precision=HIGHEST)
    acc_imag = jnp.einsum(spec_one, real_in, sin_one, precision=HIGHEST)
    if imag_part is not None:
        imag_in = imag_part.reshape(shape_in)
        acc_real = acc_real - jnp.einsum(spec_one, imag_in, sin_one, precision=HIGHEST)
        acc_imag = acc_imag + jnp.einsum(spec_one, imag_in, cos_one, precision=HIGHEST)
    twist_cos, twist_sin = section_table(outer_size, inner_size, padded, direction)
    mid_real = acc_real * twist_cos - acc_imag * twist_sin
    mid_imag = acc_real * twist_sin + acc_imag * twist_cos
    cos_two, sin_two = section_table(inner_size, inner_size // 2, inner_size, direction)
    out_real = jnp.einsum("bnq,qm->bmn", mid_real, cos_two, precision=HIGHEST) - jnp.einsum(
        "bnq,qm->bmn", mid_imag, sin_two, precision=HIGHEST
    )
    out_imag = jnp.einsum("bnq,qm->bmn", mid_real, sin_two, precision=HIGHEST) + jnp.einsum(
        "bnq,qm->bmn", mid_imag, cos_two, precision=HIGHEST
    )
    return (out_real.reshape(batch_count, extent), out_imag.reshape(batch_count, extent))


def quarter_phase(extent):
    angle_steps = lax.broadcasted_iota(jnp.int32, (1, extent), 1).astype(jnp.float32) * (
        math.pi / (2.0 * extent)
    )
    return (jnp.cos(angle_steps), jnp.sin(angle_steps))


def cosine_forward(values, batch_last):
    extent = values.shape[0] if batch_last else values.shape[1]
    spec_real, spec_imag = half_transform(values, None, -1, batch_last)
    phase_cos, phase_sin = quarter_phase(extent)
    return spec_real * phase_cos + spec_imag * phase_sin


def cosine_inverse(values, batch_last):
    extent = values.shape[0] if batch_last else values.shape[1]
    phase_cos, phase_sin = quarter_phase(extent)
    if batch_last:
        phase_cos = phase_cos.reshape(extent, 1)
        phase_sin = phase_sin.reshape(extent, 1)
    return half_transform(values * phase_cos, values * phase_sin, 1, batch_last)


def coefficient(wave_u, wave_v, grid_size):
    freq_u = wave_u * (math.pi / grid_size)
    freq_v = wave_v * (math.pi / grid_size)
    radius = freq_u * freq_u + freq_v * freq_v
    weight_u = jnp.where(wave_u == 0, 1.0 / grid_size, 2.0 / grid_size)
    weight_v = jnp.where(wave_v == 0, 1.0 / grid_size, 2.0 / grid_size)
    return jnp.where(radius > 0, weight_u * weight_v / jnp.where(radius > 0, radius, 1.0), 0.0)


def put_block(profile, offset, extent):
    relative = lax.broadcasted_iota(jnp.int32, (1, extent, 1), 1) - offset[:, None, :]
    placed = jnp.zeros(relative.shape, jnp.bfloat16)
    for step_b in range(profile.shape[0]):
        placed = placed + jnp.where(
            relative == step_b, profile[step_b][:, None, :], jnp.zeros((), jnp.bfloat16)
        )
    return placed


def tile_pieces(entry_rows, entry_cols, row_offset, col_offset, first_tile, per_group, band_rows):
    rows_part = lax.dynamic_slice_in_dim(entry_rows, first_tile, per_group, 1)
    cols_part = lax.dynamic_slice_in_dim(entry_cols, first_tile, per_group, 1)
    rows_shift = lax.dynamic_slice_in_dim(row_offset, first_tile, per_group, 0)
    cols_shift = lax.dynamic_slice_in_dim(col_offset, first_tile, per_group, 0)
    return (put_block(rows_part, rows_shift, band_rows), put_block(cols_part, cols_shift, TW))


def spread_density(entry_rows, entry_cols, row_offset, col_offset, band_rows):
    tile_count = row_offset.shape[0]
    per_group = 4

    def spread_one_group(group_index, density):
        first_tile = group_index * per_group
        tall_block, wide_block = tile_pieces(
            entry_rows, entry_cols, row_offset, col_offset, first_tile, per_group, band_rows
        )
        block_sum = jnp.einsum(
            "trk,tjk->rtj", tall_block, wide_block, preferred_element_type=jnp.float32
        )
        return lax.dynamic_update_slice_in_dim(
            density, block_sum.reshape(band_rows, per_group * TW), first_tile * TW, 1
        )

    start_value = jnp.zeros((band_rows, tile_count * TW), jnp.float32)
    return lax.fori_loop(0, tile_count // per_group, spread_one_group, start_value)


def footprint_force(fields, entry_rows, entry_cols, row_offset, col_offset, band_rows):
    tile_count = row_offset.shape[0]
    per_group = 4

    def footprint_one_group(group_index, forces):
        first_tile = group_index * per_group
        tall_block, wide_block = tile_pieces(
            entry_rows, entry_cols, row_offset, col_offset, first_tile, per_group, band_rows
        )
        field_part = lax.dynamic_slice_in_dim(fields, first_tile * TW, per_group * TW, 2).reshape(
            2, band_rows, per_group, TW
        )
        crossed = jnp.einsum(
            "frtj,tjk->ftrk", field_part, wide_block, preferred_element_type=jnp.float32
        )
        summed = jnp.sum(crossed * tall_block[None].astype(jnp.float32), axis=2)
        return lax.dynamic_update_slice_in_dim(forces, summed, first_tile, 1)

    start_value = jnp.zeros((2, tile_count, row_offset.shape[1]), jnp.float32)
    return lax.fori_loop(0, tile_count // per_group, footprint_one_group, start_value) / (BH * BW)


def per_device(row_profile, col_profile, send_list, tile_list, row_offset, col_offset, macro_mask):
    row_count = lax.axis_size("rows")
    cell_count = lax.axis_size("cells")
    devices = row_count * cell_count
    slot_count = send_list.shape[1]
    band_rows, grid_size = macro_mask.shape
    freq_dev = grid_size // devices
    own_index = lax.axis_index("rows") * cell_count + lax.axis_index("cells")
    row_height = row_profile.shape[0]
    profile_height = row_height + col_profile.shape[0]
    profiles = jnp.concatenate([row_profile, col_profile], axis=0)
    outgoing = jnp.take(profiles, send_list.reshape(-1), axis=1, mode="fill", fill_value=0)
    outgoing = outgoing.reshape(profile_height, row_count, cell_count * slot_count)
    got_profiles = lax.all_to_all(
        lax.all_to_all(outgoing, "rows", split_axis=1, concat_axis=1, tiled=True),
        "cells",
        split_axis=2,
        concat_axis=2,
        tiled=True,
    )
    got_profiles = got_profiles.reshape(profile_height, devices * slot_count)
    entries = jnp.take(got_profiles, tile_list, axis=1, mode="fill", fill_value=0)
    entry_rows = entries[:row_height]
    entry_cols = entries[row_height:]
    density = spread_density(entry_rows, entry_cols, row_offset, col_offset, band_rows)
    density = density + MACRO_LEVEL * macro_mask.astype(jnp.float32)
    along_x = cosine_forward(density, False)
    outgoing_rows = along_x.reshape(band_rows, row_count, cell_count, freq_dev).transpose(
        1, 2, 0, 3
    )
    outgoing_rows = outgoing_rows.reshape(row_count, cell_count, band_rows * freq_dev)
    columns = lax.all_to_all(
        lax.all_to_all(outgoing_rows, "rows", split_axis=0, concat_axis=0, tiled=True),
        "cells",
        split_axis=1,
        concat_axis=1,
        tiled=True,
    )
    spectrum = cosine_forward(columns.reshape(grid_size, freq_dev), True)
    wave_v = (own_index * freq_dev + lax.broadcasted_iota(jnp.int32, (freq_dev, 1), 0)).astype(
        jnp.float32
    )
    wave_u = lax.broadcasted_iota(jnp.int32, (1, grid_size), 1).astype(jnp.float32)
    scaled = spectrum * coefficient(wave_u, wave_v, grid_size)
    freq_u = wave_u * (math.pi / grid_size)
    freq_v = wave_v * (math.pi / grid_size)
    stacked = jnp.concatenate([scaled * freq_v, scaled * freq_u], axis=0)
    wave_real, wave_imag = cosine_inverse(stacked, False)
    map_stack = jnp.stack([wave_real[:freq_dev], wave_imag[freq_dev:]])
    map_count = map_stack.shape[0]
    outgoing_maps = map_stack.reshape(
        map_count, freq_dev, row_count, cell_count, band_rows
    ).transpose(0, 2, 3, 1, 4)
    outgoing_maps = outgoing_maps.reshape(map_count, row_count, cell_count, freq_dev * band_rows)
    held_maps = lax.all_to_all(
        lax.all_to_all(outgoing_maps, "rows", split_axis=1, concat_axis=1, tiled=True),
        "cells",
        split_axis=2,
        concat_axis=2,
        tiled=True,
    )
    held_maps = held_maps.reshape(map_count, grid_size, band_rows)
    x_map = held_maps[0]
    field_x = cosine_inverse(x_map, True)[1]
    field_y = cosine_inverse(held_maps[1], True)[0]
    fields = jnp.stack([field_x, field_y]).astype(jnp.bfloat16)
    forces = footprint_force(fields, entry_rows, entry_cols, row_offset, col_offset, band_rows)
    slot_forces = (
        jnp.zeros((2, devices * slot_count), jnp.float32).at[:, tile_list].add(forces, mode="drop")
    )
    returned = lax.all_to_all(
        lax.all_to_all(
            slot_forces.reshape(2, row_count, cell_count, slot_count),
            "rows",
            split_axis=1,
            concat_axis=1,
            tiled=True,
        ),
        "cells",
        split_axis=2,
        concat_axis=2,
        tiled=True,
    )
    cell_force = (
        jnp.zeros((2, row_profile.shape[1]), jnp.float32)
        .at[:, send_list]
        .add(returned.reshape(2, devices, slot_count), mode="drop")
    )
    return (fields, cell_force)


def solution(mesh):
    placed = (
        P(None, ("rows", "cells")),
        P(None, ("rows", "cells")),
        P(("rows", "cells"), None),
        P(("rows", "cells"), None),
        P(("rows", "cells"), None),
        P(("rows", "cells"), None),
        P(("rows", "cells"), None),
    )
    return jax.shard_map(
        per_device,
        mesh=mesh,
        in_specs=placed,
        out_specs=(P(None, ("rows", "cells"), None), P(None, ("rows", "cells"))),
        check_vma=False,
    )
```

profile of v0, /device:TPU:1, one launch (start us, length us, event | category | flops | bytes accessed | tf_op | source)
XLA Modules:
  0.0 458.3 jit_solution(2919077494300540546)
XLA Ops:
  3.3 29.4 %gather_fusion = bf16[8192,20]{1,0:T(8,128)(2,1)} fusion(bf16[20,4096]{0,1:T(8,128)(2,1)S(1)} %copy.325, s32[8192]{0:T(1024)S(1)} %broadcast_clamp_fusion.1), kind=kCustom, calls=%fused_computation | custom fusion | bytes 688128 | tf_op jit(solution)/shard_map/jit(_take)/gather | solution.py:160
  36.4 20.4 %all-to-all-start = ((bf16[128,2,640]{2,1,0:T(2,128)(2,1)}), bf16[128,2,640]{2,1,0:T(2,128)(2,1)S(1)}, u32[]{:S(2)}, u32[]{:S(2)}) async-start(bf16[128,2,640]{2,1,0:T(2,128)(2,1)} %reshape.453), calls=%async_computation | async-start | bytes 655360 | tf_op jit(solution)/shard_map/all_to_all | solution.py:163
  57.1 25.1 %all-to-all-done = bf16[128,2,640]{2,1,0:T(2,128)(2,1)S(1)} async-done(((bf16[128,2,640]{2,1,0:T(2,128)(2,1)}), bf16[128,2,640]{2,1,0:T(2,128)(2,1)S(1)}, u32[]{:S(2)}, u32[]{:S(2)}) %all-to-all-start) | async-done | bytes 327712 | tf_op jit(solution)/shard_map/all_to_all | solution.py:163
  84.1 4.4 all-to-all-start.1
  90.3 4.4 all-to-all-done.1
  94.7 3.5 copy.328
  98.2 29.4 %gather_fusion.1 = bf16[8192,20]{1,0:T(8,128)(2,1)} fusion(bf16[20,8192]{0,1:T(8,128)(2,1)S(1)} %bitcast.288, s32[8192]{0:T(1024)S(1)} %broadcast_clamp_fusion), kind=kCustom, calls=%fused_computation.1 | custom fusion | bytes 688128 | tf_op jit(solution)/shard_map/jit(_take)/gather | solution.py:170
  129.8 14.3 %while.30 = (s32[]{:T(128)}, f32[8,4096]{1,0:T(8,128)S(1)}, s32[32,256]{1,0:T(8,128)}, bf16[16,32,256]{2,1,0:T(8,128)(2,1)S(1)}, s32[32,256]{1,0:T(8,128)}, /*in...) while((s32[]{:T(128)}, f32[8,4096]{1,0:T(8,128)S(1)}, ...), condition=%wide.region_1.2_spmd, body=%wide.region_0.1_spmd.sunk | while | flops 10756121 | bytes 164421 | solution.py:124
  153.2 3.5 add_bitcast_fusion
  159.7 8.8 %all-to-all-start.2 = ((f32[128,1,256]{2,1,0:T(1,128)}), f32[128,1,256]{2,1,0:T(1,128)S(1)}, u32[]{:S(2)}, u32[]{:S(2)}) async-start(f32[128,1,256]{2,1,0:T(1,128)} %reshape.455), calls=%async_computation.2 | async-start | bytes 262144 | tf_op jit(solution)/shard_map/all_to_all | solution.py:181
  168.7 17.0 %all-to-all-done.2 = f32[128,1,256]{2,1,0:T(1,128)S(1)} async-done(((f32[128,1,256]{2,1,0:T(1,128)}), f32[128,1,256]{2,1,0:T(1,128)S(1)}, u32[]{:S(2)}, u32[]{:S(2)}) %all-to-all-start.2) | async-done | bytes 131104 | tf_op jit(solution)/shard_map/all_to_all | solution.py:181
  191.4 4.8 %all-to-all-done.3 = f32[128,4,64]{0,2,1:T(8,128)S(1)} async-done(((f32[128,4,64]{0,2,1:T(8,128)}), f32[128,4,64]{0,2,1:T(8,128)S(1)}, u32[]{:S(2)}, u32[]{:S(2)}) %all-to-all-start.3) | async-done | bytes 131104 | tf_op jit(solution)/shard_map/all_to_all | solution.py:180
  220.8 4.6 %maximum_bitcast_fusion = f32[2,128,4,8,8]{4,2,1,3,0:T(4,128)} fusion(f32[1,8,128,4,8]{4,3,2,1,0:T(4,128)} %stack.14, f32[1,8,128,4,8]{4,3,2,1,0:T(4,128)S(1)} %stack.13), kind=kLoop, calls=%fused_computation.330 | loop fusion | flops 65536 | bytes 524288 | tf_op jit(solution)/shard_map/transpose | solution.py:201
  229.6 30.1 %all_to_all.40 = f32[128,1,512]{2,1,0:T(1,128)S(1)} all-to-all(f32[128,1,512]{2,1,0:T(1,128)S(1)} %reshape.457), channel_id=1, replica_groups=mesh['rows'=128,'cells'=4] {'rows'}, dimensions={0} | all-to-all | bytes 524288 | tf_op jit(solution)/shard_map/all_to_all | solution.py:204
  262.1 3.6 all-to-all-start.5
  265.7 5.5 %all-to-all-done.5 = f32[2,128,4,64]{1,3,0,2:T(8,128)S(1)} async-done(((f32[2,128,4,64]{1,3,0,2:T(8,128)}), f32[2,128,4,64]{1,3,0,2:T(8,128)S(1)}, u32[]{:S(2)}, u32[]{:S(2)}) %all-to-all-start.5) | async-done | bytes 262176 | tf_op jit(solution)/shard_map/all_to_all | solution.py:203
  275.5 4.9 %broadcast_multiply_fusion.1 = (f32[32,128,8]{2,1,0:T(8,128)S(1)}, f32[32,128,8]{2,1,0:T(8,128)}, f32[32,128,8]{2,1,0:T(8,128)}, f32[32,128,8]{2,1,0:T(8,128)}) fusion(f32[32,128,8]{2,1,0:T(8,128)} %squeeze.126, f32[32,128]{1,0:T(8,128)S(1)} %get-tuple-element.442, f32[32,128]{1,0:T(8,128)S(1)} %get-tuple-element.443, f32[32,128,8]{2,1,0:T(8,128)} %squeeze.127), kind=kLoop, calls=%fused_computation.361 | loop fusion | flops 131072 | bytes 819200 | tf_op jit(solution)/shard_map/mul | solution.py:77
  299.2 20.9 %while.31 = (s32[]{:T(128)}, f32[2,32,256]{2,0,1:T(2,128)S(1)}, s32[32,256]{1,0:T(8,128)}, bf16[16,32,256]{2,1,0:T(8,128)(2,1)S(1)}, bf16[2,8,4096]{2,1,0:T(8,12...) while((s32[]{:T(128)}, f32[2,32,256]{2,0,1:T(2,128)S(1)}, ...), condition=%wide.region_4.5_spmd, body=%wide.region_2.4_spmd.sunk | while | flops 12883993 | bytes 254545 | solution.py:146
  322.7 46.7 %scatter_custom_fusion = f32[2,8192]{0,1:T(8,128)} fusion(s32[8192]{0:T(1024)S(1)} %bitcast.302, f32[8192,2]{1,0:T(8,128)} %copy.354, f32[]{:T(128)} %constant.546.clone.1), kind=kCustom, calls=%fused_computation.331 | custom fusion | flops 16384 | bytes 66048 | tf_op jit(solution)/shard_map/scatter-add | solution.py:217
  369.4 4.8 %copy.355 = f32[2,128,4,16]{3,2,0,1:T(4,128)S(1)} copy(f32[2,128,4,16]{0,3,2,1:T(8,128)} %bitcast.287) | data formatting | bytes 131072 | tf_op jit(solution)/shard_map/reshape | solution.py:221
  374.6 22.9 %all_to_all.41 = f32[128,1,128]{2,1,0:T(1,128)S(1)} all-to-all(f32[128,1,128]{2,1,0:T(1,128)S(1)} %reshape.459), channel_id=1, replica_groups=mesh['rows'=128,'cells'=4] {'rows'}, dimensions={0} | all-to-all | bytes 131072 | tf_op jit(solution)/shard_map/all_to_all | solution.py:220
  403.1 4.1 all-to-all-done.7
  407.5 4.5 copy.360
  412.0 44.8 %scatter_custom_fusion.1 = f32[2,4096]{0,1:T(8,128)S(1)} fusion(s32[8192]{0:T(1024)S(1)} %reshape.429, f32[8192,2]{1,0:T(8,128)} %bitcast.289, f32[]{:T(128)} %constant.546.clone.1), kind=kCustom, calls=%fused_computation.358 | custom fusion | flops 16384 | bytes 33280 | tf_op jit(solution)/shard_map/scatter-add | solution.py:235
  (199 shorter events, 129.1 us)
Async XLA Ops:
  34.9 22.1 %copy-start.5 = (s32[32,256]{1,0:T(8,128)S(1)}, s32[32,256]{1,0:T(8,128)}, u32[]{:S(2)}) copy-start(s32[32,256]{1,0:T(8,128)} %param.14) | copy-start | bytes 98308
  36.4 45.8 %all-to-all-start = ((bf16[128,2,640]{2,1,0:T(2,128)(2,1)}), bf16[128,2,640]{2,1,0:T(2,128)(2,1)S(1)}, u32[]{:S(2)}, u32[]{:S(2)}) async-start(bf16[128,2,640]{2,1,0:T(2,128)(2,1)} %reshape.453), calls=%async_computation | async-start | bytes 655360 | tf_op jit(solution)/shard_map/all_to_all | solution.py:163
  84.1 10.6 %all-to-all-start.1 = ((bf16[20,128,64]{1,0,2:T(8,128)(2,1)}), bf16[20,128,64]{1,0,2:T(8,128)(2,1)S(1)}, u32[]{:S(2)}, u32[]{:S(2)}) async-start(bf16[20,128,64]{1,0,2:T(8,128)(2,1)} %copy.327), calls=%async_computation.1 | async-start | bytes 786432 | tf_op jit(solution)/shard_map/all_to_all | solution.py:162
  129.8 14.4 %copy-start.3 = (s32[8,4096]{1,0:T(8,128)S(1)}, s32[8,4096]{1,0:T(8,128)}, u32[]{:S(2)}) copy-start(s32[8,4096]{1,0:T(8,128)} %param.17) | copy-start | bytes 393220
  144.1 1.0 copy-start.2
  150.5 2.8 copy-start
  150.5 2.8 copy-start.1
  159.7 26.1 %all-to-all-start.2 = ((f32[128,1,256]{2,1,0:T(1,128)}), f32[128,1,256]{2,1,0:T(1,128)S(1)}, u32[]{:S(2)}, u32[]{:S(2)}) async-start(f32[128,1,256]{2,1,0:T(1,128)} %reshape.455), calls=%async_computation.2 | async-start | bytes 262144 | tf_op jit(solution)/shard_map/all_to_all | solution.py:181
  188.0 8.1 %all-to-all-start.3 = ((f32[128,4,64]{0,2,1:T(8,128)}), f32[128,4,64]{0,2,1:T(8,128)S(1)}, u32[]{:S(2)}, u32[]{:S(2)}) async-start(f32[128,4,64]{0,2,1:T(8,128)} %copy.336), calls=%async_computation.3 | async-start | bytes 262144 | tf_op jit(solution)/shard_map/all_to_all | solution.py:180
  262.1 9.1 %all-to-all-start.5 = ((f32[2,128,4,64]{1,3,0,2:T(8,128)}), f32[2,128,4,64]{1,3,0,2:T(8,128)S(1)}, u32[]{:S(2)}, u32[]{:S(2)}) async-start(f32[2,128,4,64]{1,3,0,2:T(8,128)} %copy.342), calls=%async_computation.5 | async-start | bytes 524288 | tf_op jit(solution)/shard_map/all_to_all | solution.py:203
  320.0 2.7 copy-start.6
  374.2 28.6 %copy-start.4 = (s32[512,16]{0,1:T(8,128)S(1)}, s32[512,16]{0,1:T(8,128)}, u32[]{:S(2)}) copy-start(s32[512,16]{0,1:T(8,128)} %param.13) | copy-start | bytes 98308
  399.5 7.7 %all-to-all-start.7 = ((f32[2,128,4,16]{1,3,0,2:T(8,128)}), f32[2,128,4,16]{1,3,0,2:T(8,128)S(1)}, u32[]{:S(2)}, u32[]{:S(2)}) async-start(f32[2,128,4,16]{1,3,0,2:T(8,128)} %copy.356), calls=%async_computation.7 | async-start | bytes 131072 | tf_op jit(solution)/shard_map/all_to_all | solution.py:219
where the time goes:
time: 465 us; the launch traced here: 458 us
  local copies, waits for them, and re-layouts  141 us (30%)
  other arithmetic  109 us (23%)
  waiting for transfers between devices  60.9 us (13%)
  blocking collectives  53.1 us (11%)
  matrix products  48.5 us (10%)
  starting transfers between devices  43.7 us (9%)
    scatter-add x1, other arithmetic, per_device(): jnp.zeros((2, devices * slot_count), jnp.float32).at[:, tile_list]  46.7 us
    scatter-add x1, other arithmetic, per_device(): cell_force = jnp.zeros((2, row_profile.shape[1]), jnp.float32).at[:, send...  44.8 us
    gather x2, local copies, waits for them, and re-layouts, per_device(): jnp.take(profiles, send_list.reshape(-1), axis=1, mode='fill', fill_value=0)  31.6 us
    gather x2, local copies, waits for them, and re-layouts, per_device(): jnp.take(got_profiles, tile_list, axis=1, mode='fill', fill_value=0)  31.5 us
    all_to_all x1, blocking collectives, per_device(): lax.all_to_all(outgoing_maps, 'rows', split_axis=1, concat_axis=1, tiled=...  30.1 us
    all_to_all x1, waiting for transfers between devices, per_device(): lax.all_to_all(outgoing, 'rows', split_axis=1, concat_axis=1, tiled=True)  25.1 us
    all_to_all x1, blocking collectives, per_device(): lax.all_to_all(slot_forces.reshape(2, row_count, cell_count, slot_count),...  22.9 us
    all_to_all x1, starting transfers between devices, per_device(): lax.all_to_all(outgoing, 'rows', split_axis=1, concat_axis=1, tiled=True)  20.4 us
  transfers between devices with their start and end apart: 6, of which 6 were waited for; matrix products, arithmetic and copies ran while one was open for 1% of the time, Pallas kernels for 0%

commit v1 on v0

v1 whole, which is shorter than its diff:
```python
import functools
import math

import jax
import jax.numpy as jnp
import numpy as np
from jax import lax
from jax.experimental import pallas as pl
from jax.experimental.pallas import tpu as pltpu
from jax.sharding import Mesh
from jax.sharding import PartitionSpec as P

GRID = 4096
BH = 4
BW = 16
TW = 128
TH = 8
NT = 32
TCAP = 256
CAP = 16
CELL_DEV = 4096
LOW = 256
MACRO_LEVEL = 4.0
SCALE = 8192.0
F32 = jnp.float32
BF16 = jnp.bfloat16
I32 = jnp.int32


def split_host(values):
    top = values.astype(jnp.bfloat16)
    rest = (values - top.astype(np.float64)).astype(jnp.bfloat16)
    return top, rest


@functools.cache
def tables_x():
    q = np.arange(512) // 128
    r = (np.arange(512) % 128) // 16
    f = 16 * q + np.arange(512) % 16
    t = np.arange(256) // 8
    r_in = np.arange(256) % 8
    same = r_in[:, None] == r[None, :]
    turn = np.pi * ((t[:, None] * f[None, :]) % 64) / 32.0
    first = np.concatenate([np.cos(turn) * same, -np.sin(turn) * same], axis=1)
    b = np.arange(128)
    angle = np.pi * (f[None, :] * (2 * b[:, None] + 1)) / 8192.0
    w = np.arange(64)
    wave = np.pi * ((w[:, None] * (2 * b[None, :] + 1)) % 256) / 128.0
    second = np.concatenate([np.cos(wave), np.sin(wave)], axis=1)
    return (
        split_host(first),
        np.cos(angle).astype(np.float32),
        np.sin(angle).astype(np.float32),
        split_host(second),
    )


@functools.cache
def tables_y():
    lane = np.arange(128)
    r, c, l = lane // 16, (lane // 8) % 2, lane % 8
    f = np.arange(128)
    a = np.arange(64)
    turn = np.pi * ((f[:, None] * a[None, :]) % 128) / 64.0
    first = np.concatenate([np.cos(turn), -np.sin(turn)], axis=0)
    h = np.arange(4)
    b = 32 * c[None, :] + 8 * h[:, None] + r[None, :]
    angle = np.pi * (f[None, :, None] * (2 * b[:, None, :] + 1)) / 8192.0
    w = np.arange(256) // 8
    l_out = np.arange(256) % 8
    wave = np.pi * (((2 * b[:, :, None] + 1) * w[None, None, :]) % 128) / 64.0
    same = l[:, None] == l_out[None, :]
    second = np.stack([np.cos(wave) * same[None], np.sin(wave) * same[None]], axis=1)
    return (
        split_host(first),
        np.cos(angle).astype(np.float32),
        np.sin(angle).astype(np.float32),
        split_host(second.reshape(1024, 256)),
    )


def halves(values):
    top = values.astype(BF16)
    return top, (values - top.astype(F32)).astype(BF16)


def dot(left, right):
    return jnp.dot(left, right, preferred_element_type=F32)


def dot_last(left, right):
    return lax.dot_general(left, right, (((1,), (1,)), ((), ())), preferred_element_type=F32)


def dot3(left, right):
    left_top, left_rest = left
    right_top, right_rest = right
    return dot(left_top, right_top) + (dot(left_rest, right_top) + dot(left_top, right_rest))


def one_hot(index_row, extent):
    lines = lax.broadcasted_iota(I32, (extent, index_row.shape[1]), 0)
    return jnp.where(lines == index_row, 1.0, 0.0).astype(BF16)


def join_cores(own, other, core):
    lane_core = (lax.broadcasted_iota(I32, own.shape, 1) // 8) % 2
    moved = jnp.where(core == 0, pltpu.roll(other, 8, 1), pltpu.roll(other, 120, 1))
    return jnp.where(lane_core == core, own, moved)


def pack_kernel(row_ref, col_ref, list_ref, out_ref, low_ref, high_ref, table, cols, rows):
    core = lax.axis_index("c")
    for h in range(16):
        table[h * 16 : h * 16 + 16, :] = col_ref[:, h * LOW : (h + 1) * LOW]
    table[256:320, :] = jnp.concatenate(
        [row_ref[:, h * LOW : (h + 1) * LOW].astype(F32) for h in range(16)], axis=0
    ).astype(BF16)
    listed = list_ref[...].astype(F32).T
    high = jnp.floor(listed * (1.0 / LOW))
    low = listed - high * LOW
    target = lax.broadcasted_iota(I32, (512, 512), 1)
    source = (target % 256) // 4 * 8 + ((target // 256) ^ core) * 4 + target % 4
    move = jnp.where(lax.broadcasted_iota(I32, (512, 512), 0) == source, 1.0, 0.0).astype(BF16)
    high_ref[...] = dot(high.astype(BF16), move).astype(I32)
    low_ref[...] = dot(low.astype(BF16), move).astype(I32)
    upper = lax.broadcasted_iota(I32, (8, 512), 0) // 4

    def pick(k):
        found = dot(table[...], one_hot(low_ref[pl.ds(k, 1), :], LOW))
        place = jnp.broadcast_to(high_ref[pl.ds(k, 1), :], (8, 512))
        col_sum = [jnp.zeros((8, 512), F32) for _ in range(2)]
        for h in range(16):
            here = place == h
            for s in range(2):
                start = h * 16 + s * 8
                col_sum[s] = col_sum[s] + jnp.where(here, found[start : start + 8], 0.0)
        row_sum = jnp.zeros((8, 512), F32)
        for h in range(8):
            start = 256 + h * 8
            row_sum = row_sum + jnp.where(place == 2 * h + upper, found[start : start + 8], 0.0)
        row_sum = row_sum + pltpu.roll(row_sum, 4, 0)
        col_sum = jnp.concatenate(col_sum, axis=0)
        return (col_sum * SCALE).astype(I32), (row_sum * SCALE).astype(I32)

    def step(j, carry):
        row_words = []
        for s in range(2):
            k = 2 * j + s
            col_a, row_a = pick(k)
            col_b, row_b = pick(k + 8)
            cols[pl.ds(pl.multiple_of(k * 16, 16), 16), :] = col_a + (col_b << 16)
            row_words.append(row_a + (row_b << 16))
        rows[pl.ds(pl.multiple_of(j * 8, 8), 8), :] = jnp.where(
            upper == 0, row_words[0], row_words[1]
        )
        return carry

    lax.fori_loop(0, 4, step, 0)
    for c in range(2):
        out_ref[pl.ds(c, 256, stride=3), :] = cols[:, c * 256 : (c + 1) * 256].T
    both = [rows[:, :256], rows[:, 256:]]
    out_ref[pl.ds(2, 256, stride=3), :] = jnp.concatenate(both + both, axis=0).T


def pack_profiles(row_profile, col_profile, send_list):
    return pl.pallas_call(
        pack_kernel,
        out_shape=(
            jax.ShapeDtypeStruct((768, 128), I32),
            jax.ShapeDtypeStruct((16, 512), I32),
            jax.ShapeDtypeStruct((16, 512), I32),
        ),
        scratch_shapes=[
            pltpu.VMEM((320, 256), BF16),
            pltpu.VMEM((128, 512), I32),
            pltpu.VMEM((32, 512), I32),
        ],
        compiler_params=pltpu.CompilerParams(vmem_limit_bytes=32 << 20),
        name="pack_profiles",
    )(row_profile, col_profile, send_list)


def slot_address(slots, core):
    source = slots // 16
    low = source // 8 * 4 + source % 4
    high = (((source // 4) % 2) ^ core) * 16 + slots % 16
    return low, high


def spread_kernel(
    own_ref,
    other_ref,
    list_ref,
    row_ref,
    col_ref,
    mask_ref,
    first_top,
    first_rest,
    turn_cos,
    turn_sin,
    second_top,
    second_rest,
    out_ref,
    wide_ref,
    tall_ref,
    low_ref,
    high_ref,
    table,
    density,
):
    core = lax.axis_index("c")
    for s, ref in enumerate((own_ref, other_ref)):
        words = ref[pl.ds(s, 256, stride=3), :].T
        for part, piece in enumerate((words & 0xFFFF, words >> 16)):
            start = s * 256 + part * 128
            table[start : start + 128, :] = (piece.astype(F32) * (1.0 / SCALE)).astype(BF16)
    own_rows = own_ref[pl.ds(2, 256, stride=3), :].T
    other_rows = other_ref[pl.ds(2, 256, stride=3), :].T
    words = jnp.concatenate([own_rows[:32], other_rows[32:64]], axis=0)
    for part, piece in enumerate((words & 0xFFFF, words >> 16)):
        start = 512 + part * 64
        table[start : start + 64, :] = (piece.astype(F32) * (1.0 / SCALE)).astype(BF16)
    low, high = slot_address(list_ref[...], core)
    low_ref[...] = low
    high_ref[...] = high
    upper = lax.broadcasted_iota(I32, (8, TCAP), 0) // 4

    def step(t, carry):
        found = dot(table[...], one_hot(low_ref[pl.ds(t, 1), :], LOW))
        place = jnp.broadcast_to(high_ref[pl.ds(t, 1), :], (8, TCAP))
        col_sum = [jnp.zeros((8, TCAP), F32) for _ in range(2)]
        for h in range(32):
            here = place == h
            for s in range(2):
                start = h * 16 + s * 8
                col_sum[s] = col_sum[s] + jnp.where(here, found[start : start + 8], 0.0)
        row_sum = jnp.zeros((8, TCAP), F32)
        for part in range(2):
            for s in range(2):
                for j in range(4):
                    start = 512 + part * 64 + s * 32 + j * 8
                    here = place == s * 16 + part * 8 + j * 2 + upper
                    row_sum = row_sum + jnp.where(here, found[start : start + 8], 0.0)
        row_sum = row_sum + pltpu.roll(row_sum, 4, 0)
        tall = jnp.where(upper == 0, row_sum, 0.0)
        row_shift = jnp.broadcast_to(row_ref[pl.ds(t, 1), :], (8, TCAP))
        for shift in (1, 2, 4):
            tall = jnp.where((row_shift & shift) != 0, pltpu.roll(tall, shift, 0), tall)
        col_shift = jnp.broadcast_to(col_ref[pl.ds(t, 1), :], (8, TCAP))
        zero = jnp.zeros((8, TCAP), F32)
        strip = jnp.concatenate(col_sum + [zero], axis=0)
        for shift in (1, 2, 4):
            moves = (col_shift & shift) != 0
            moved = pltpu.roll(strip, shift, 0)
            strip = jnp.concatenate(
                [
                    jnp.where(moves, moved[i * 8 : i * 8 + 8], strip[i * 8 : i * 8 + 8])
                    for i in range(3)
                ],
                axis=0,
            )
        blocks = [strip[i * 8 : i * 8 + 8] for i in range(3)]
        for shift in (1, 2, 4, 8):
            moves = (col_shift & (8 * shift)) != 0
            held = blocks
            blocks = []
            for i in range(min(16, len(held) + shift)):
                stay = held[i] if i < len(held) else zero
                come = held[i - shift] if i >= shift else zero
                blocks.append(jnp.where(moves, come, stay))
        wide = jnp.concatenate(blocks, axis=0).astype(BF16)
        wide_ref[pl.ds(pl.multiple_of(t * 128, 128), 128), :] = wide
        tall_ref[pl.ds(pl.multiple_of(t * 8, 8), 8), :] = tall
        covered = mask_ref[:, pl.ds(pl.multiple_of(t * 128, 128), 128)].astype(F32)
        density[pl.ds(pl.multiple_of(t * 8, 8), 8), :] = (
            dot_last(tall.astype(BF16), wide) + MACRO_LEVEL * covered
        )
        return carry

    lax.fori_loop(0, NT, step, 0)
    turned = halves(density[...].T)
    mixed = dot3(turned, (first_top[...], first_rest[...]))
    real, imag = mixed[:, :512], mixed[:, 512:]
    cos, sin = turn_cos[...], turn_sin[...]
    stacked = jnp.concatenate([real * cos + imag * sin, imag * cos - real * sin], axis=0)
    result = dot3((second_top[...], second_rest[...]), halves(stacked))
    for q in range(4):
        out_ref[q * 64 : q * 64 + 64, :] = result[:, q * 128 : q * 128 + 128]


def spread(own, other, tile_list, row_offset, col_offset, macro_mask):
    first, cos, sin, second = tables_x()
    return pl.pallas_call(
        spread_kernel,
        out_shape=(
            jax.ShapeDtypeStruct((256, 128), F32),
            jax.ShapeDtypeStruct((NT * TW, TCAP), BF16),
            jax.ShapeDtypeStruct((NT * TH, TCAP), F32),
            jax.ShapeDtypeStruct((NT, TCAP), I32),
            jax.ShapeDtypeStruct((NT, TCAP), I32),
        ),
        scratch_shapes=[pltpu.VMEM((640, 256), BF16), pltpu.VMEM((NT * TH, TW), F32)],
        compiler_params=pltpu.CompilerParams(vmem_limit_bytes=40 << 20),
        name="spread",
    )(own, other, tile_list, row_offset, col_offset, macro_mask, *first, cos, sin, *second)


def solve_kernel(
    own_ref,
    other_ref,
    first_top,
    first_rest,
    back_top,
    back_rest,
    turn_cos,
    turn_sin,
    second_top,
    second_rest,
    wave_top,
    wave_rest,
    out_ref,
    held,
):
    core = lax.axis_index("c")
    place = (lax.axis_index("x") * 16 + lax.axis_index("z")) * 4 + lax.axis_index("y")
    held[...] = join_cores(own_ref[...], other_ref[...], core)
    first = (first_top[...], first_rest[...])
    parts = []
    for h in range(4):
        mixed = dot3(first, halves(held[pl.ds(h, 64, stride=4), :]))
        real, imag = mixed[:128], mixed[128:]
        cos, sin = turn_cos[h], turn_sin[h]
        parts += [real * cos + imag * sin, imag * cos - real * sin]
    spectrum = dot3(halves(jnp.concatenate(parts, axis=1)), (second_top[...], second_rest[...]))
    lane = lax.broadcasted_iota(I32, (128, 256), 1)
    wave_u = lax.broadcasted_iota(I32, (128, 256), 0) + 128 * (lane // 8)
    wave_v = (place // 64) * 16 + core * 8 + lane % 8 + 64 * (place % 64)
    freq_u = wave_u.astype(F32) * (math.pi / GRID)
    freq_v = wave_v.astype(F32) * (math.pi / GRID)
    radius = freq_u * freq_u + freq_v * freq_v
    weight_u = jnp.where(wave_u == 0, 1.0 / GRID, 2.0 / GRID)
    weight_v = jnp.where(wave_v == 0, 1.0 / GRID, 2.0 / GRID)
    kernel = jnp.where(
        radius > 0, weight_u * weight_v / jnp.where(radius > 0, radius, 1.0), 0.0
    )
    scaled = spectrum * kernel
    both = jnp.concatenate([scaled * freq_v, scaled * freq_u], axis=0)
    waves = dot3(halves(both), (wave_top[...], wave_rest[...]))
    back = (back_top[...], back_rest[...])
    for h in range(4):
        cos, sin = turn_cos[h], turn_sin[h]
        maps = []
        for m in range(2):
            rows = slice(m * 128, m * 128 + 128)
            real = waves[rows, h * 256 : h * 256 + 128]
            imag = waves[rows, h * 256 + 128 : h * 256 + 256]
            out_real = real * cos - imag * sin
            out_imag = real * sin + imag * cos
            pair = [out_real, out_imag] if m == 0 else [out_imag, -out_real]
            maps.append(jnp.concatenate(pair, axis=0))
        result = dot3(back, halves(jnp.concatenate(maps, axis=1)))
        for m in range(2):
            out_ref[pl.ds(2 * h + m, 64, stride=8), :] = result[:, m * 128 : m * 128 + 128]


def solve_columns(own, other):
    first, cos, sin, second = tables_y()
    back = tuple(np.ascontiguousarray(part.T) for part in first)
    wave = tuple(np.ascontiguousarray(part.T) for part in second)
    return pl.pallas_call(
        solve_kernel,
        out_shape=jax.ShapeDtypeStruct((512, 128), F32),
        scratch_shapes=[pltpu.VMEM((256, 128), F32)],
        compiler_params=pltpu.CompilerParams(vmem_limit_bytes=40 << 20),
        name="solve_columns",
    )(own, other, *first, *back, cos, sin, *second, *wave)


def force_kernel(
    own_ref,
    other_ref,
    wide_ref,
    tall_ref,
    low_ref,
    high_ref,
    wave_top,
    wave_rest,
    turn_cos,
    turn_sin,
    last_top,
    last_rest,
    fields_ref,
    out_ref,
    held,
    field,
    total,
):
    core = lax.axis_index("c")
    held[...] = join_cores(own_ref[...], other_ref[...], core)
    columns = [
        held[pl.ds(q * 128 + m, 64, stride=2), :] for m in range(2) for q in range(4)
    ]
    waves = dot3((wave_top[...], wave_rest[...]), halves(jnp.concatenate(columns, axis=1)))
    cos, sin = turn_cos[...], turn_sin[...]
    maps = []
    for m in range(2):
        real = waves[:128, m * 512 : m * 512 + 512]
        imag = waves[128:, m * 512 : m * 512 + 512]
        out_real = real * cos - imag * sin
        out_imag = real * sin + imag * cos
        pair = [out_imag, -out_real] if m == 0 else [out_real, out_imag]
        maps.append(jnp.concatenate(pair, axis=1))
    result = dot3(halves(jnp.concatenate(maps, axis=0)), (last_top[...], last_rest[...]))
    field[...] = result.T
    total[...] = jnp.zeros_like(total)
    lines = lax.broadcasted_iota(I32, (32, TCAP), 0)

    def step(t, carry):
        here = pl.ds(pl.multiple_of(t * 8, 8), 8)
        tile = field[here, :]
        pair = jnp.concatenate([tile[:, :128], tile[:, 128:]], axis=0).astype(BF16)
        for m in range(2):
            fields_ref[m, :, pl.ds(pl.multiple_of(t * 128, 128), 128)] = pair[
                m * 8 : m * 8 + 8
            ]
        wide = wide_ref[pl.ds(pl.multiple_of(t * 128, 128), 128), :]
        crossed = dot(pair, wide)
        tall = tall_ref[here, :]
        chosen = lines == high_ref[pl.ds(t, 1), :]
        tops, rests = [], []
        for m in range(2):
            force = jnp.sum(crossed[m * 8 : m * 8 + 8] * tall, axis=0, keepdims=True) * (
                1.0 / (BH * BW)
            )
            top = force.astype(BF16).astype(F32)
            tops.append(jnp.where(chosen, top, 0.0))
            rests.append(jnp.where(chosen, force - top, 0.0))
        left = jnp.concatenate(tops + rests, axis=0).astype(BF16)
        total[...] += dot_last(left, one_hot(low_ref[pl.ds(t, 1), :], LOW))
        return carry

    lax.fori_loop(0, NT, step, 0)
    summed = total[:64, :] + total[64:, :]
    out_ref[...] = jnp.concatenate([summed, summed], axis=0).T


def tile_forces(own, other, wide, tall, low, high):
    last, cos, sin, wave = tables_x()
    last = tuple(np.ascontiguousarray(part.T) for part in last)
    wave = tuple(np.ascontiguousarray(part.T) for part in wave)
    return pl.pallas_call(
        force_kernel,
        out_shape=(
            jax.ShapeDtypeStruct((2, TH, GRID), BF16),
            jax.ShapeDtypeStruct((256, 128), F32),
        ),
        scratch_shapes=[
            pltpu.VMEM((512, 128), F32),
            pltpu.VMEM((256, 256), F32),
            pltpu.VMEM((128, 256), F32),
        ],
        compiler_params=pltpu.CompilerParams(vmem_limit_bytes=40 << 20),
        name="tile_forces",
    )(own, other, wide, tall, low, high, *wave, cos, sin, *last)


def gather_kernel(own_ref, other_ref, low_ref, high_ref, out_ref, own, other, total):
    own[...] = own_ref[...].T
    other[...] = other_ref[...].T
    total[...] = jnp.zeros_like(total)
    lines = lax.broadcasted_iota(I32, (16, 512), 0)

    def step(k, carry):
        chosen = lines == high_ref[pl.ds(k, 1), :]
        tops, rests = [], []
        for m in range(2):
            force = jnp.concatenate(
                [own[pl.ds(m * 32 + k, 1), :], other[pl.ds(m * 32 + 16 + k, 1), :]], axis=1
            )
            top = force.astype(BF16).astype(F32)
            tops.append(jnp.where(chosen, top, 0.0))
            rests.append(jnp.where(chosen, force - top, 0.0))
        left = jnp.concatenate(tops + rests, axis=0).astype(BF16)
        total[...] += dot_last(left, one_hot(low_ref[pl.ds(k, 1), :], LOW))
        return carry

    lax.fori_loop(0, CAP, step, 0)
    summed = total[:32, :] + total[32:, :]
    for m in range(2):
        for h in range(16):
            out_ref[m : m + 1, h * LOW : (h + 1) * LOW] = summed[m * 16 + h : m * 16 + h + 1]


def gather_forces(own, other, low, high):
    return pl.pallas_call(
        gather_kernel,
        out_shape=jax.ShapeDtypeStruct((2, CELL_DEV), F32),
        scratch_shapes=[
            pltpu.VMEM((128, 256), F32),
            pltpu.VMEM((128, 256), F32),
            pltpu.VMEM((64, 256), F32),
        ],
        compiler_params=pltpu.CompilerParams(vmem_limit_bytes=32 << 20),
        name="gather_forces",
    )(own, other, low, high)


def exchange(words):
    rows = words.shape[0]
    sent = words.reshape(256, 1, rows // 256 * 128)
    own = lax.all_to_all(sent, ("x", "z", "y"), split_axis=0, concat_axis=0, tiled=True)
    own = own.reshape(rows, 128)
    return own, lax.ppermute(own, "c", [(0, 1), (1, 0)])


def per_device(row_profile, col_profile, send_list, tile_list, row_offset, col_offset, macro_mask):
    words, cell_low, cell_high = pack_profiles(row_profile, col_profile, send_list)
    own, other = exchange(words)
    lines, wide, tall, slot_low, slot_high = spread(
        own, other, tile_list, row_offset, col_offset, macro_mask
    )
    maps = solve_columns(*exchange(lines))
    fields, forces = tile_forces(*exchange(maps), wide, tall, slot_low, slot_high)
    cell_force = gather_forces(*exchange(forces), cell_low, cell_high)
    return (fields, cell_force)


def solution(mesh):
    fine = Mesh(mesh.devices.reshape(4, 16, 2, 4), ("x", "z", "c", "y"))
    every = ("x", "z", "c", "y")
    placed = (P(None, every), P(None, every)) + (P(every, None),) * 5
    return jax.shard_map(
        per_device,
        mesh=fine,
        in_specs=placed,
        out_specs=(P(None, every, None), P(None, every)),
        check_vma=False,
    )
```

time: 465 us -> 209 us (0.45); the launches traced: 458 us -> 208 us
  local copies, waits for them, and re-layouts: 141 us -> 11.3 us
  other arithmetic: 109 us -> 0 us
  blocking collectives: 53.1 us -> 140 us
  waiting for transfers between devices: 60.9 us -> 4.4 us
  matrix products: 48.5 us -> 0 us
  Pallas kernels: 0 us -> 35.3 us
  starting transfers between devices: 43.7 us -> 15.2 us
    scatter-add x2 -> x0, other arithmetic: 91.5 us -> none  [the longest x1 46.7 us: per_device(): jnp.zeros((2, devices * slot_count), jnp.float32).at[:, tile_list]]
    all_to_all x2 -> x4, blocking collectives: 53.1 us -> 140 us  [exchange(): lax.all_to_all(sent, ('x', 'z', 'y'), split_axis=0, concat_axis=0, tiled=...]
    gather x4 -> x0, local copies, waits for them, and re-layouts: 63.1 us -> none  [the longest x2 31.6 us: per_device(): jnp.take(profiles, send_list.reshape(-1), axis=1, mode='fill', fill_value=0)]
    all_to_all x6 -> x0, waiting for transfers between devices: 60.9 us -> none  [the longest x1 25.1 us: per_device(): lax.all_to_all(outgoing, 'rows', split_axis=1, concat_axis=1, tiled=True)]
    all_to_all x6 -> x0, starting transfers between devices: 43.7 us -> none  [the longest x1 20.4 us: per_device(): lax.all_to_all(outgoing, 'rows', split_axis=1, concat_axis=1, tiled=True)]
    dot_general x40 -> x0, matrix products: 40.4 us -> none  [the longest x8 8.04 us: spread_one_group(): jnp.einsum('trk,tjk->rtj', tall_block, wide_block, preferred_element_type...]
    pallas_call x0 -> x5, Pallas kernels: none -> 35.3 us  [the longest x1 14.6 us: spread(): pl.pallas_call(spread_kernel, out_shape=(jax.ShapeDtypeStruct((256, 128),...]
    ppermute x0 -> x4, starting transfers between devices: none -> 15.2 us  [exchange(): return (own, lax.ppermute(own, 'c', [(0, 1), (1, 0)]))]
  transfers between devices with their start and end apart: 6 -> 4, of which waited for: 6 -> 4; matrix products, arithmetic and copies ran while one was open for 1% -> 0% of each run, Pallas kernels for 0% -> 0%
where the time goes in v1:
time: 209 us; the launch traced here: 208 us
  blocking collectives  140 us (67%)
  Pallas kernels  35.3 us (17%)
  starting transfers between devices  15.2 us (7%)
  local copies, waits for them, and re-layouts  11.3 us (5%)
  waiting for transfers between devices  4.4 us (2%)
    all_to_all x4, blocking collectives, exchange(): lax.all_to_all(sent, ('x', 'z', 'y'), split_axis=0, concat_axis=0, tiled=...  140 us
    ppermute x4, starting transfers between devices, exchange(): return (own, lax.ppermute(own, 'c', [(0, 1), (1, 0)]))  15.2 us
    pallas_call x1, Pallas kernels, spread(): pl.pallas_call(spread_kernel, out_shape=(jax.ShapeDtypeStruct((256, 128),...  14.6 us
    pallas_call x1, Pallas kernels, tile_forces(): pl.pallas_call(force_kernel, out_shape=(jax.ShapeDtypeStruct((2, TH, GRID...  11.5 us
    unnamed x57, local copies, waits for them, and re-layouts  11.3 us
    ppermute x4, waiting for transfers between devices, exchange(): return (own, lax.ppermute(own, 'c', [(0, 1), (1, 0)]))  4.4 us
  transfers between devices with their start and end apart: 4, of which 4 were waited for; matrix products, arithmetic and copies ran while one was open for 0% of the time, Pallas kernels for 0%

profile of v1, /device:TPU:1, one launch (start us, length us, event | category | flops | bytes accessed | tf_op | source)
XLA Modules:
  0.0 207.6 jit_solution(1004031617293878143)
XLA Ops:
  0.7 0.9 copy.30.list_ref
  1.6 0.9 copy-done.14
  3.3 2.9 %pack_profiles.1 = (s32[768,128]{1,0:T(8,128)S(1)}, s32[16,512]{1,0:T(8,128)S(1)}, s32[16,512]{1,0:T(8,128)S(1)}) custom-call(bf16[4,4096]{1,0:T(4,128)(2,1)S(1)} %copy-done.22, bf16[16,4096]{1,0:T(8,128)(2,1)S(1)} %copy-done.14, s32[512,16]{1,0:T(8,128)S(1)} %copy.30.list_ref), custom_call_target="tpu_custom_call" | custom-call | tf_op jit(solution)/shard_map/pack_profiles/pallas_call | solution.py:168
  6.1 53.5 %all_to_all.20 = s32[256,1,384]{2,1,0:T(1,128)S(1)} all-to-all(s32[256,1,384]{2,1,0:T(1,128)S(1)} %bitcast.21), channel_id=1, replica_groups=mesh['x'=4,'z'=16,'c'=2,'y'=4] {'x','z','y'}, dimensions={0} | all-to-all | bytes 786432 | tf_op jit(solution)/shard_map/all_to_all | solution.py:513
  59.6 4.6 %collective-permute-start = (s32[768,128]{1,0:T(8,128)S(1)}, s32[768,128]{1,0:T(8,128)S(1)}, u32[]{:S(2)}, u32[]{:S(2)}) collective-permute-start(s32[768,128]{1,0:T(8,128)S(1)} %bitcast.12), channel_id=1, source_target_pairs={{0,4},{4,0},{1,5},{5,1},{2,6},{6,2},{3,7},{7,3},{8,12},{12,8},{9,1... | collective-permute-start | bytes 1179656 | tf_op jit(solution)/shard_map/ppermute | solution.py:515
  64.2 1.3 collective-permute-done.other_ref
  65.6 0.9 copy-done
  66.5 0.9 copy-done.2
  67.5 1.0 copy-done.10
  68.5 1.0 copy-done.11
  69.5 0.9 copy-done.15
  74.2 14.6 %spread.1 = (f32[256,128]{1,0:T(8,128)S(1)}, bf16[4096,256]{1,0:T(8,128)(2,1)S(1)}, f32[256,256]{1,0:T(8,128)S(1)}, s32[32,256]{1,0:T(8,128)S(1)}, s32[32,256]{1,0:T(8,128)S(1)}) custom-call(s32[768,128]{1,0:T(8,128)S(1)} %bitcast.13, s32[768,128]{1,0:T(8,128)S(1)} %collective-permute-done.other_ref, s32[32,256]{1,0:T(8,128)S(1)} %copy-done.23, ...), custom_call_target="tpu_custom_call" | custom-call | tf_op jit(solution)/shard_map/spread/pallas_call | solution.py:295
  88.9 27.1 %all_to_all.21 = f32[256,1,128]{2,1,0:T(1,128)S(1)} all-to-all(f32[256,1,128]{2,1,0:T(1,128)S(1)} %bitcast.23), channel_id=1, replica_groups=mesh['x'=4,'z'=16,'c'=2,'y'=4] {'x','z','y'}, dimensions={0} | all-to-all | bytes 262144 | tf_op jit(solution)/shard_map/all_to_all | solution.py:513
  116.0 3.6 %collective-permute-start.1 = (f32[256,128]{1,0:T(8,128)S(1)}, f32[256,128]{1,0:T(8,128)S(1)}, u32[]{:S(2)}, u32[]{:S(2)}) collective-permute-start(f32[256,128]{1,0:T(8,128)S(1)} %bitcast.17), channel_id=1, source_target_pairs={{0,4},{4,0},{1,5},{5,1},{2,6},{6,2},{3,7},{7,3},{8,12},{12,8},{9,1... | collective-permute-start | bytes 393224 | tf_op jit(solution)/shard_map/ppermute | solution.py:515
  119.6 1.0 collective-permute-done.1.other_ref
  120.6 2.2 %solve_columns.1 = f32[512,128]{1,0:T(8,128)S(1)} custom-call(f32[256,128]{1,0:T(8,128)S(1)} %bitcast.18, f32[256,128]{1,0:T(8,128)S(1)} %collective-permute-done.1.other_ref, bf16[256,64]{1,0:T(8,128)(2,1)S(1)} %copy-done.19, bf16[256,64]{1,0:T(8,128)(2,1)S(1)} %copy-done.18, bf16[64,256]{1,0:T(8,128)(2,1)S(1)} %copy-done.21, ...), custom_call_target="tpu_custom_call" | custom-call | tf_op jit(solution)/shard_map/solve_columns/pallas_call | solution.py:372
  122.9 32.9 %all_to_all.22 = f32[256,1,256]{2,1,0:T(1,128)S(1)} all-to-all(f32[256,1,256]{2,1,0:T(1,128)S(1)} %bitcast.16), channel_id=1, replica_groups=mesh['x'=4,'z'=16,'c'=2,'y'=4] {'x','z','y'}, dimensions={0} | all-to-all | bytes 524288 | tf_op jit(solution)/shard_map/all_to_all | solution.py:513
  155.7 3.5 %collective-permute-start.2 = (f32[512,128]{1,0:T(8,128)S(1)}, f32[512,128]{1,0:T(8,128)S(1)}, u32[]{:S(2)}, u32[]{:S(2)}) collective-permute-start(f32[512,128]{1,0:T(8,128)S(1)} %bitcast.14), channel_id=1, source_target_pairs={{0,4},{4,0},{1,5},{5,1},{2,6},{6,2},{3,7},{7,3},{8,12},{12,8},{9,1... | collective-permute-start | bytes 786440 | tf_op jit(solution)/shard_map/ppermute | solution.py:515
  159.3 1.1 collective-permute-done.2.other_ref
  160.4 11.5 %tile_forces.1 = (bf16[2,8,4096]{2,1,0:T(8,128)(2,1)}, f32[256,128]{1,0:T(8,128)S(1)}) custom-call(f32[512,128]{1,0:T(8,128)S(1)} %bitcast.15, f32[512,128]{1,0:T(8,128)S(1)} %collective-permute-done.2.other_ref, bf16[4096,256]{1,0:T(8,128)(2,1)S(1)} %get-tuple-element.14.wide_ref, f32[256,256]{1,0:T(8,128)S(1)} %get-tuple-element.15.tall_ref, ...), custom_call_target="tpu_custom_call" | custom-call | tf_op jit(solution)/shard_map/tile_forces/pallas_call | solution.py:453
  172.0 27.0 %all_to_all.23 = f32[256,1,128]{2,1,0:T(1,128)S(1)} all-to-all(f32[256,1,128]{2,1,0:T(1,128)S(1)} %bitcast.22), channel_id=1, replica_groups=mesh['x'=4,'z'=16,'c'=2,'y'=4] {'x','z','y'}, dimensions={0} | all-to-all | bytes 262144 | tf_op jit(solution)/shard_map/all_to_all | solution.py:513
  199.0 3.6 %collective-permute-start.3 = (f32[256,128]{1,0:T(8,128)S(1)}, f32[256,128]{1,0:T(8,128)S(1)}, u32[]{:S(2)}, u32[]{:S(2)}) collective-permute-start(f32[256,128]{1,0:T(8,128)S(1)} %bitcast.19), channel_id=1, source_target_pairs={{0,4},{4,0},{1,5},{5,1},{2,6},{6,2},{3,7},{7,3},{8,12},{12,8},{9,1... | collective-permute-start | bytes 393224 | tf_op jit(solution)/shard_map/ppermute | solution.py:515
  202.5 1.0 collective-permute-done.3.other_ref
  203.5 4.1 %gather_forces.1 = f32[2,4096]{1,0:T(2,128)} custom-call(f32[256,128]{1,0:T(8,128)S(1)} %bitcast.20, f32[256,128]{1,0:T(8,128)S(1)} %collective-permute-done.3.other_ref, s32[16,512]{1,0:T(8,128)S(1)} %get-tuple-element.20.low_ref, s32[16,512]{1,0:T(8,128)S(1)} %get-tuple-element.21.high_ref), custom_call_target="tpu_custom_call" | custom-call | tf_op jit(solution)/shard_map/gather_forces/pallas_call | solution.py:497
  (50 shorter events, 4.6 us)
Async XLA Ops:
  0.6 119.9 %copy-start.12 = (f32[4,128,128]{2,1,0:T(8,128)S(1)}, f32[4,128,128]{2,1,0:T(8,128)}, u32[]{:S(2)}) copy-start(f32[4,128,128]{2,1,0:T(8,128)} %constant.51.clone.turn_sin) | copy-start | bytes 786436
  0.6 119.9 %copy-start.21 = (bf16[64,256]{1,0:T(8,128)(2,1)S(1)}, bf16[64,256]{1,0:T(8,128)(2,1)}, u32[]{:S(2)}) copy-start(bf16[64,256]{1,0:T(8,128)(2,1)} %constant.48.clone.back_top) | copy-start | bytes 98308
  3.2 117.3 %copy-start.6 = (bf16[256,1024]{1,0:T(8,128)(2,1)S(1)}, bf16[256,1024]{1,0:T(8,128)(2,1)}, u32[]{:S(2)}) copy-start(bf16[256,1024]{1,0:T(8,128)(2,1)} %constant.55.clone.wave_rest) | copy-start | bytes 1572868
  3.3 117.3 %copy-start.7 = (bf16[256,1024]{1,0:T(8,128)(2,1)S(1)}, bf16[256,1024]{1,0:T(8,128)(2,1)}, u32[]{:S(2)}) copy-start(bf16[256,1024]{1,0:T(8,128)(2,1)} %constant.54.clone.wave_top) | copy-start | bytes 1572868
  3.3 117.3 %copy-start.18 = (bf16[256,64]{1,0:T(8,128)(2,1)S(1)}, bf16[256,64]{1,0:T(8,128)(2,1)}, u32[]{:S(2)}) copy-start(bf16[256,64]{1,0:T(8,128)(2,1)} %constant.47.clone.first_rest) | copy-start | bytes 98308
  3.3 117.3 %copy-start.19 = (bf16[256,64]{1,0:T(8,128)(2,1)S(1)}, bf16[256,64]{1,0:T(8,128)(2,1)}, u32[]{:S(2)}) copy-start(bf16[256,64]{1,0:T(8,128)(2,1)} %constant.46.clone.first_top) | copy-start | bytes 98308
  3.3 117.3 %copy-start.20 = (bf16[64,256]{1,0:T(8,128)(2,1)S(1)}, bf16[64,256]{1,0:T(8,128)(2,1)}, u32[]{:S(2)}) copy-start(bf16[64,256]{1,0:T(8,128)(2,1)} %constant.49.clone.back_rest) | copy-start | bytes 98308
  59.6 5.9 %collective-permute-start = (s32[768,128]{1,0:T(8,128)S(1)}, s32[768,128]{1,0:T(8,128)S(1)}, u32[]{:S(2)}, u32[]{:S(2)}) collective-permute-start(s32[768,128]{1,0:T(8,128)S(1)} %bitcast.12), channel_id=1, source_target_pairs={{0,4},{4,0},{1,5},{5,1},{2,6},{6,2},{3,7},{7,3},{8,12},{12,8},{9,1... | collective-permute-start | bytes 1179656 | tf_op jit(solution)/shard_map/ppermute | solution.py:515
  65.6 0.9 copy-start
  66.5 0.9 copy-start.2
  67.5 1.0 copy-start.10
  68.5 1.0 copy-start.11
  74.2 46.4 %copy-start.8 = (bf16[1024,256]{1,0:T(8,128)(2,1)S(1)}, bf16[1024,256]{1,0:T(8,128)(2,1)}, u32[]{:S(2)}) copy-start(bf16[1024,256]{1,0:T(8,128)(2,1)} %constant.53.clone.second_rest) | copy-start | bytes 1572868
  74.2 46.4 %copy-start.9 = (bf16[1024,256]{1,0:T(8,128)(2,1)S(1)}, bf16[1024,256]{1,0:T(8,128)(2,1)}, u32[]{:S(2)}) copy-start(bf16[1024,256]{1,0:T(8,128)(2,1)} %constant.52.clone.second_top) | copy-start | bytes 1572868
  74.2 46.4 %copy-start.13 = (f32[4,128,128]{2,1,0:T(8,128)S(1)}, f32[4,128,128]{2,1,0:T(8,128)}, u32[]{:S(2)}) copy-start(f32[4,128,128]{2,1,0:T(8,128)} %constant.50.clone.turn_cos) | copy-start | bytes 786436
  88.8 71.6 %copy-start.1 = (f32[128,512]{1,0:T(8,128)S(1)}, f32[128,512]{1,0:T(8,128)}, u32[]{:S(2)}) copy-start(f32[128,512]{1,0:T(8,128)} %constant.43.clone.turn_sin) | copy-start | bytes 786436
  88.8 71.6 %copy-start.3 = (f32[128,512]{1,0:T(8,128)S(1)}, f32[128,512]{1,0:T(8,128)}, u32[]{:S(2)}) copy-start(f32[128,512]{1,0:T(8,128)} %constant.42.clone.turn_cos) | copy-start | bytes 786436
  88.8 71.6 %copy-start.4 = (bf16[1024,256]{1,0:T(8,128)(2,1)S(1)}, bf16[1024,256]{1,0:T(8,128)(2,1)}, u32[]{:S(2)}) copy-start(bf16[1024,256]{1,0:T(8,128)(2,1)} %constant.59.clone.last_rest) | copy-start | bytes 1572868
  88.8 71.6 %copy-start.5 = (bf16[1024,256]{1,0:T(8,128)(2,1)S(1)}, bf16[1024,256]{1,0:T(8,128)(2,1)}, u32[]{:S(2)}) copy-start(bf16[1024,256]{1,0:T(8,128)(2,1)} %constant.58.clone.last_top) | copy-start | bytes 1572868
  88.9 71.6 %copy-start.16 = (bf16[256,64]{1,0:T(8,128)(2,1)S(1)}, bf16[256,64]{1,0:T(8,128)(2,1)}, u32[]{:S(2)}) copy-start(bf16[256,64]{1,0:T(8,128)(2,1)} %constant.57.clone.wave_rest) | copy-start | bytes 98308
  88.9 71.6 %copy-start.17 = (bf16[256,64]{1,0:T(8,128)(2,1)S(1)}, bf16[256,64]{1,0:T(8,128)(2,1)}, u32[]{:S(2)}) copy-start(bf16[256,64]{1,0:T(8,128)(2,1)} %constant.56.clone.wave_top) | copy-start | bytes 98308
  116.0 4.5 %collective-permute-start.1 = (f32[256,128]{1,0:T(8,128)S(1)}, f32[256,128]{1,0:T(8,128)S(1)}, u32[]{:S(2)}, u32[]{:S(2)}) collective-permute-start(f32[256,128]{1,0:T(8,128)S(1)} %bitcast.17), channel_id=1, source_target_pairs={{0,4},{4,0},{1,5},{5,1},{2,6},{6,2},{3,7},{7,3},{8,12},{12,8},{9,1... | collective-permute-start | bytes 393224 | tf_op jit(solution)/shard_map/ppermute | solution.py:515
  155.7 4.7 %collective-permute-start.2 = (f32[512,128]{1,0:T(8,128)S(1)}, f32[512,128]{1,0:T(8,128)S(1)}, u32[]{:S(2)}, u32[]{:S(2)}) collective-permute-start(f32[512,128]{1,0:T(8,128)S(1)} %bitcast.14), channel_id=1, source_target_pairs={{0,4},{4,0},{1,5},{5,1},{2,6},{6,2},{3,7},{7,3},{8,12},{12,8},{9,1... | collective-permute-start | bytes 786440 | tf_op jit(solution)/shard_map/ppermute | solution.py:515
  199.0 4.6 %collective-permute-start.3 = (f32[256,128]{1,0:T(8,128)S(1)}, f32[256,128]{1,0:T(8,128)S(1)}, u32[]{:S(2)}, u32[]{:S(2)}) collective-permute-start(f32[256,128]{1,0:T(8,128)S(1)} %bitcast.19), channel_id=1, source_target_pairs={{0,4},{4,0},{1,5},{5,1},{2,6},{6,2},{3,7},{7,3},{8,12},{12,8},{9,1... | collective-permute-start | bytes 393224 | tf_op jit(solution)/shard_map/ppermute | solution.py:515
  (8 other events, 6.4 us)

commit v2 on v1

--- a/solution.py
+++ b/solution.py
@@ -22,6 +22,9 @@
 LOW = 256
 MACRO_LEVEL = 4.0
 SCALE = 8192.0
+SPREAD_GROUP = 16
+FORCE_GROUP = 16
+GATHER_GROUP = 16
 F32 = jnp.float32
 BF16 = jnp.bfloat16
 I32 = jnp.int32
@@ -100,8 +103,31 @@
 
 
 def one_hot(index_row, extent):
-    lines = lax.broadcasted_iota(I32, (extent, index_row.shape[1]), 0)
-    return jnp.where(lines == index_row, 1.0, 0.0).astype(BF16)
+    shape = (extent, index_row.shape[1])
+    lines = lax.broadcasted_iota(I32, shape, 0).astype(BF16)
+    index = jnp.broadcast_to(index_row.astype(BF16), shape)
+    return jnp.where(lines == index, jnp.ones(shape, BF16), jnp.zeros(shape, BF16))
+
+
+def choose(blocks, index):
+    bit = 1
+    while len(blocks) > 1:
+        odd = (index & bit) != 0
+        blocks = [
+            jnp.where(odd, blocks[2 * i + 1], blocks[2 * i]) for i in range(len(blocks) // 2)
+        ]
+        bit *= 2
+    return blocks[0]
+
+
+def load_all(pairs, sems):
+    copies = [
+        pltpu.make_async_copy(source, target, sems.at[i])
+        for i, (source, target) in enumerate(pairs)
+    ]
+    for copy in copies:
+        copy.start()
+    return copies
 
 
 def join_cores(own, other, core):
@@ -110,38 +136,41 @@
     return jnp.where(lane_core == core, own, moved)
 
 
-def pack_kernel(row_ref, col_ref, list_ref, out_ref, low_ref, high_ref, table, cols, rows):
+def pack_kernel(
+    row_hbm, col_hbm, list_ref, out_ref, low_ref, high_ref, row_ref, col_ref, table, cols, rows, sems
+):
     core = lax.axis_index("c")
+    copies = load_all([(col_hbm, col_ref), (row_hbm, row_ref)], sems)
+    listed = list_ref[...].astype(F32)
+    empty = listed >= CELL_DEV
+    high = jnp.floor(listed * (1.0 / LOW))
+    low = jnp.where(empty, float(LOW), listed - high * LOW)
+    target = lax.broadcasted_iota(I32, (512, 512), 1)
+    source = (target % 256) // 4 * 8 + ((target // 256) ^ core) * 4 + target % 4
+    move = jnp.where(lax.broadcasted_iota(I32, (512, 512), 0) == source, 1.0, 0.0).astype(BF16)
+    high_ref[...] = dot(high.astype(BF16), move).astype(I32)
+    low_ref[...] = dot(low.astype(BF16), move).astype(I32)
+    for copy in copies:
+        copy.wait()
     for h in range(16):
         table[h * 16 : h * 16 + 16, :] = col_ref[:, h * LOW : (h + 1) * LOW]
     table[256:320, :] = jnp.concatenate(
         [row_ref[:, h * LOW : (h + 1) * LOW].astype(F32) for h in range(16)], axis=0
     ).astype(BF16)
-    listed = list_ref[...].astype(F32).T
-    high = jnp.floor(listed * (1.0 / LOW))
-    low = listed - high * LOW
-    target = lax.broadcasted_iota(I32, (512, 512), 1)
-    source = (target % 256) // 4 * 8 + ((target // 256) ^ core) * 4 + target % 4
-    move = jnp.where(lax.broadcasted_iota(I32, (512, 512), 0) == source, 1.0, 0.0).astype(BF16)
-    high_ref[...] = dot(high.astype(BF16), move).astype(I32)
-    low_ref[...] = dot(low.astype(BF16), move).astype(I32)
     upper = lax.broadcasted_iota(I32, (8, 512), 0) // 4
 
     def pick(k):
         found = dot(table[...], one_hot(low_ref[pl.ds(k, 1), :], LOW))
         place = jnp.broadcast_to(high_ref[pl.ds(k, 1), :], (8, 512))
-        col_sum = [jnp.zeros((8, 512), F32) for _ in range(2)]
-        for h in range(16):
-            here = place == h
-            for s in range(2):
-                start = h * 16 + s * 8
-                col_sum[s] = col_sum[s] + jnp.where(here, found[start : start + 8], 0.0)
-        row_sum = jnp.zeros((8, 512), F32)
-        for h in range(8):
-            start = 256 + h * 8
-            row_sum = row_sum + jnp.where(place == 2 * h + upper, found[start : start + 8], 0.0)
-        row_sum = row_sum + pltpu.roll(row_sum, 4, 0)
-        col_sum = jnp.concatenate(col_sum, axis=0)
+        col_sum = jnp.concatenate(
+            [
+                choose([found[h * 16 + s * 8 : h * 16 + s * 8 + 8] for h in range(16)], place)
+                for s in range(2)
+            ],
+            axis=0,
+        )
+        row_sum = choose([found[256 + h * 8 : 264 + h * 8] for h in range(8)], place // 2)
+        row_sum = jnp.where(place % 2 == upper, row_sum, pltpu.roll(row_sum, 4, 0))
         return (col_sum * SCALE).astype(I32), (row_sum * SCALE).astype(I32)
 
     def step(j, carry):
@@ -153,15 +182,19 @@
             cols[pl.ds(pl.multiple_of(k * 16, 16), 16), :] = col_a + (col_b << 16)
             row_words.append(row_a + (row_b << 16))
         rows[pl.ds(pl.multiple_of(j * 8, 8), 8), :] = jnp.where(
-            upper == 0, row_words[0], row_words[1]
+            upper == 0, row_words[0], pltpu.roll(row_words[1], 4, 0)
         )
         return carry
 
-    lax.fori_loop(0, 4, step, 0)
+    lax.fori_loop(0, 4, step, 0, unroll=True)
     for c in range(2):
         out_ref[pl.ds(c, 256, stride=3), :] = cols[:, c * 256 : (c + 1) * 256].T
     both = [rows[:, :256], rows[:, 256:]]
     out_ref[pl.ds(2, 256, stride=3), :] = jnp.concatenate(both + both, axis=0).T
+
+
+HBM = pl.BlockSpec(memory_space=pltpu.HBM)
+VMEM = pl.BlockSpec(memory_space=pltpu.VMEM)
 
 
 def pack_profiles(row_profile, col_profile, send_list):
@@ -172,14 +205,18 @@
             jax.ShapeDtypeStruct((16, 512), I32),
             jax.ShapeDtypeStruct((16, 512), I32),
         ),
+        in_specs=[HBM, HBM, VMEM],
         scratch_shapes=[
+            pltpu.VMEM((BH, CELL_DEV), BF16),
+            pltpu.VMEM((BW, CELL_DEV), BF16),
             pltpu.VMEM((320, 256), BF16),
             pltpu.VMEM((128, 512), I32),
             pltpu.VMEM((32, 512), I32),
+            pltpu.SemaphoreType.DMA((2,)),
         ],
         compiler_params=pltpu.CompilerParams(vmem_limit_bytes=32 << 20),
         name="pack_profiles",
-    )(row_profile, col_profile, send_list)
+    )(row_profile, col_profile, send_list.T)
 
 
 def slot_address(slots, core):
@@ -192,6 +229,21 @@
 def spread_kernel(
     own_ref,
     other_ref,
+    list_hbm,
+    row_hbm,
+    col_hbm,
+    mask_hbm,
+    first_top_hbm,
+    first_rest_hbm,
+    turn_cos_hbm,
+    turn_sin_hbm,
+    second_top_hbm,
+    second_rest_hbm,
+    out_ref,
+    wide_ref,
+    tall_ref,
+    low_ref,
+    high_ref,
     list_ref,
     row_ref,
     col_ref,
@@ -202,15 +254,26 @@
     turn_sin,
     second_top,
     second_rest,
-    out_ref,
-    wide_ref,
-    tall_ref,
-    low_ref,
-    high_ref,
     table,
     density,
+    sems,
 ):
     core = lax.axis_index("c")
+    copies = load_all(
+        [
+            (list_hbm, list_ref),
+            (row_hbm, row_ref),
+            (col_hbm, col_ref),
+            (mask_hbm, mask_ref),
+            (first_top_hbm, first_top),
+            (first_rest_hbm, first_rest),
+            (turn_cos_hbm, turn_cos),
+            (turn_sin_hbm, turn_sin),
+            (second_top_hbm, second_top),
+            (second_rest_hbm, second_rest),
+        ],
+        sems,
+    )
     for s, ref in enumerate((own_ref, other_ref)):
         words = ref[pl.ds(s, 256, stride=3), :].T
         for part, piece in enumerate((words & 0xFFFF, words >> 16)):
@@ -222,46 +285,39 @@
     for part, piece in enumerate((words & 0xFFFF, words >> 16)):
         start = 512 + part * 64
         table[start : start + 64, :] = (piece.astype(F32) * (1.0 / SCALE)).astype(BF16)
+    for copy in copies[:4]:
+        copy.wait()
     low, high = slot_address(list_ref[...], core)
     low_ref[...] = low
     high_ref[...] = high
     upper = lax.broadcasted_iota(I32, (8, TCAP), 0) // 4
-
-    def step(t, carry):
+    zero = jnp.zeros((8, TCAP), F32)
+
+    def tile(t):
         found = dot(table[...], one_hot(low_ref[pl.ds(t, 1), :], LOW))
         place = jnp.broadcast_to(high_ref[pl.ds(t, 1), :], (8, TCAP))
-        col_sum = [jnp.zeros((8, TCAP), F32) for _ in range(2)]
-        for h in range(32):
-            here = place == h
-            for s in range(2):
-                start = h * 16 + s * 8
-                col_sum[s] = col_sum[s] + jnp.where(here, found[start : start + 8], 0.0)
-        row_sum = jnp.zeros((8, TCAP), F32)
-        for part in range(2):
-            for s in range(2):
+        strip = [
+            choose([found[h * 16 + s * 8 : h * 16 + s * 8 + 8] for h in range(32)], place)
+            for s in range(2)
+        ] + [zero]
+        row_blocks = []
+        for s in range(2):
+            for part in range(2):
                 for j in range(4):
                     start = 512 + part * 64 + s * 32 + j * 8
-                    here = place == s * 16 + part * 8 + j * 2 + upper
-                    row_sum = row_sum + jnp.where(here, found[start : start + 8], 0.0)
-        row_sum = row_sum + pltpu.roll(row_sum, 4, 0)
+                    row_blocks.append(found[start : start + 8])
+        row_sum = choose(row_blocks, place // 2)
+        row_sum = jnp.where(place % 2 == upper, row_sum, pltpu.roll(row_sum, 4, 0))
         tall = jnp.where(upper == 0, row_sum, 0.0)
         row_shift = jnp.broadcast_to(row_ref[pl.ds(t, 1), :], (8, TCAP))
         for shift in (1, 2, 4):
             tall = jnp.where((row_shift & shift) != 0, pltpu.roll(tall, shift, 0), tall)
         col_shift = jnp.broadcast_to(col_ref[pl.ds(t, 1), :], (8, TCAP))
-        zero = jnp.zeros((8, TCAP), F32)
-        strip = jnp.concatenate(col_sum + [zero], axis=0)
         for shift in (1, 2, 4):
             moves = (col_shift & shift) != 0
-            moved = pltpu.roll(strip, shift, 0)
-            strip = jnp.concatenate(
-                [
-                    jnp.where(moves, moved[i * 8 : i * 8 + 8], strip[i * 8 : i * 8 + 8])
-                    for i in range(3)
-                ],
-                axis=0,
-            )
-        blocks = [strip[i * 8 : i * 8 + 8] for i in range(3)]
+            moved = pltpu.roll(jnp.concatenate(strip, axis=0), shift, 0)
+            strip = [jnp.where(moves, moved[i * 8 : i * 8 + 8], strip[i]) for i in range(3)]
+        blocks = strip
         for shift in (1, 2, 4, 8):
             moves = (col_shift & (8 * shift)) != 0
             held = blocks
@@ -270,16 +326,23 @@
                 stay = held[i] if i < len(held) else zero
                 come = held[i - shift] if i >= shift else zero
                 blocks.append(jnp.where(moves, come, stay))
-        wide = jnp.concatenate(blocks, axis=0).astype(BF16)
-        wide_ref[pl.ds(pl.multiple_of(t * 128, 128), 128), :] = wide
-        tall_ref[pl.ds(pl.multiple_of(t * 8, 8), 8), :] = tall
-        covered = mask_ref[:, pl.ds(pl.multiple_of(t * 128, 128), 128)].astype(F32)
-        density[pl.ds(pl.multiple_of(t * 8, 8), 8), :] = (
-            dot_last(tall.astype(BF16), wide) + MACRO_LEVEL * covered
-        )
+        return tall, jnp.concatenate(blocks, axis=0).astype(BF16)
+
+    def step(group, carry):
+        made = [tile(group * SPREAD_GROUP + i) for i in range(SPREAD_GROUP)]
+        for i, (tall, wide) in enumerate(made):
+            t = group * SPREAD_GROUP + i
+            wide_ref[pl.ds(pl.multiple_of(t * 128, 128), 128), :] = wide
+            tall_ref[pl.ds(pl.multiple_of(t * 8, 8), 8), :] = tall
+            covered = mask_ref[:, pl.ds(pl.multiple_of(t * 128, 128), 128)].astype(F32)
+            density[pl.ds(pl.multiple_of(t * 8, 8), 8), :] = (
+                dot_last(tall.astype(BF16), wide) + MACRO_LEVEL * covered
+            )
         return carry
 
-    lax.fori_loop(0, NT, step, 0)
+    lax.fori_loop(0, NT // SPREAD_GROUP, step, 0)
+    for copy in copies[4:]:
+        copy.wait()
     turned = halves(density[...].T)
     mixed = dot3(turned, (first_top[...], first_rest[...]))
     real, imag = mixed[:, :512], mixed[:, 512:]
@@ -292,6 +355,7 @@
 
 def spread(own, other, tile_list, row_offset, col_offset, macro_mask):
     first, cos, sin, second = tables_x()
+    loaded = (tile_list, row_offset, col_offset, macro_mask, *first, cos, sin, *second)
     return pl.pallas_call(
         spread_kernel,
         out_shape=(
@@ -301,10 +365,16 @@
             jax.ShapeDtypeStruct((NT, TCAP), I32),
             jax.ShapeDtypeStruct((NT, TCAP), I32),
         ),
-        scratch_shapes=[pltpu.VMEM((640, 256), BF16), pltpu.VMEM((NT * TH, TW), F32)],
+        in_specs=[VMEM, VMEM] + [HBM] * len(loaded),
+        scratch_shapes=[pltpu.VMEM(array.shape, array.dtype) for array in loaded]
+        + [
+            pltpu.VMEM((640, 256), BF16),
+            pltpu.VMEM((NT * TH, TW), F32),
+            pltpu.SemaphoreType.DMA((len(loaded),)),
+        ],
         compiler_params=pltpu.CompilerParams(vmem_limit_bytes=40 << 20),
         name="spread",
-    )(own, other, tile_list, row_offset, col_offset, macro_mask, *first, cos, sin, *second)
+    )(own, other, *loaded)
 
 
 def solve_kernel(
@@ -417,16 +487,11 @@
     total[...] = jnp.zeros_like(total)
     lines = lax.broadcasted_iota(I32, (32, TCAP), 0)
 
-    def step(t, carry):
+    def weights(t):
         here = pl.ds(pl.multiple_of(t * 8, 8), 8)
         tile = field[here, :]
         pair = jnp.concatenate([tile[:, :128], tile[:, 128:]], axis=0).astype(BF16)
-        for m in range(2):
-            fields_ref[m, :, pl.ds(pl.multiple_of(t * 128, 128), 128)] = pair[
-                m * 8 : m * 8 + 8
-            ]
-        wide = wide_ref[pl.ds(pl.multiple_of(t * 128, 128), 128), :]
-        crossed = dot(pair, wide)
+        crossed = dot(pair, wide_ref[pl.ds(pl.multiple_of(t * 128, 128), 128), :])
         tall = tall_ref[here, :]
         chosen = lines == high_ref[pl.ds(t, 1), :]
         tops, rests = [], []
@@ -438,10 +503,22 @@
             tops.append(jnp.where(chosen, top, 0.0))
             rests.append(jnp.where(chosen, force - top, 0.0))
         left = jnp.concatenate(tops + rests, axis=0).astype(BF16)
-        total[...] += dot_last(left, one_hot(low_ref[pl.ds(t, 1), :], LOW))
+        return pair, left, one_hot(low_ref[pl.ds(t, 1), :], LOW)
+
+    def step(group, carry):
+        tiles = [group * FORCE_GROUP + i for i in range(FORCE_GROUP)]
+        made = [weights(t) for t in tiles]
+        for t, (pair, _, _) in zip(tiles, made):
+            for m in range(2):
+                fields_ref[m, :, pl.ds(pl.multiple_of(t * 128, 128), 128)] = pair[
+                    m * 8 : m * 8 + 8
+                ]
+        left = jnp.concatenate([part[1] for part in made], axis=1)
+        right = jnp.concatenate([part[2] for part in made], axis=1)
+        total[...] += dot_last(left, right)
         return carry
 
-    lax.fori_loop(0, NT, step, 0)
+    lax.fori_loop(0, NT // FORCE_GROUP, step, 0)
     summed = total[:64, :] + total[64:, :]
     out_ref[...] = jnp.concatenate([summed, summed], axis=0).T
 
@@ -472,7 +549,7 @@
     total[...] = jnp.zeros_like(total)
     lines = lax.broadcasted_iota(I32, (16, 512), 0)
 
-    def step(k, carry):
+    def weights(k):
         chosen = lines == high_ref[pl.ds(k, 1), :]
         tops, rests = [], []
         for m in range(2):
@@ -483,10 +560,16 @@
             tops.append(jnp.where(chosen, top, 0.0))
             rests.append(jnp.where(chosen, force - top, 0.0))
         left = jnp.concatenate(tops + rests, axis=0).astype(BF16)
-        total[...] += dot_last(left, one_hot(low_ref[pl.ds(k, 1), :], LOW))
+        return left, one_hot(low_ref[pl.ds(k, 1), :], LOW)
+
+    def step(group, carry):
+        made = [weights(group * GATHER_GROUP + i) for i in range(GATHER_GROUP)]
+        left = jnp.concatenate([part[0] for part in made], axis=1)
+        right = jnp.concatenate([part[1] for part in made], axis=1)
+        total[...] += dot_last(left, right)
         return carry
 
-    lax.fori_loop(0, CAP, step, 0)
+    lax.fori_loop(0, CAP // GATHER_GROUP, step, 0)
     summed = total[:32, :] + total[32:, :]
     for m in range(2):
         for h in range(16):

time: 209 us -> 190 us (0.909)
  Pallas kernels: 35.3 us -> 16.6 us
    pallas_call x1, Pallas kernels: 14.6 us -> 5.8 us  [spread(): pl.pallas_call(spread_kernel, out_shape=(jax.ShapeDtypeStruct((256, 128),...]
    pallas_call x1, Pallas kernels: 11.5 us -> 4.24 us  [tile_forces(): pl.pallas_call(force_kernel, out_shape=(jax.ShapeDtypeStruct((2, TH, GRID...]
    pallas_call x1, Pallas kernels: 4.14 us -> 2.02 us  [gather_forces(): pl.pallas_call(gather_kernel, out_shape=jax.ShapeDtypeStruct((2, CELL_DEV...]
    unnamed x57 -> x58, local copies, waits for them, and re-layouts: 11.3 us -> 11.2 us
where the time goes in v2:
time: 190 us; the launch traced here: 189 us
  blocking collectives  140 us (74%)
  Pallas kernels  16.6 us (9%)
  starting transfers between devices  15.2 us (8%)
  local copies, waits for them, and re-layouts  11.2 us (6%)
  waiting for transfers between devices  4.4 us (2%)
    all_to_all x4, blocking collectives, exchange(): lax.all_to_all(sent, ('x', 'z', 'y'), split_axis=0, concat_axis=0, tiled=...  140 us
    ppermute x4, starting transfers between devices, exchange(): return (own, lax.ppermute(own, 'c', [(0, 1), (1, 0)]))  15.2 us
    unnamed x58, local copies, waits for them, and re-layouts  11.2 us
    pallas_call x1, Pallas kernels, spread(): pl.pallas_call(spread_kernel, out_shape=(jax.ShapeDtypeStruct((256, 128),...  5.8 us
    ppermute x4, waiting for transfers between devices, exchange(): return (own, lax.ppermute(own, 'c', [(0, 1), (1, 0)]))  4.4 us
    pallas_call x1, Pallas kernels, tile_forces(): pl.pallas_call(force_kernel, out_shape=(jax.ShapeDtypeStruct((2, TH, GRID...  4.24 us
  transfers between devices with their start and end apart: 4, of which 4 were waited for; matrix products, arithmetic and copies ran while one was open for 0% of the time, Pallas kernels for 0%

profile of v2, /device:TPU:1, one launch (start us, length us, event | category | flops | bytes accessed | tf_op | source)
XLA Modules:
  0.0 188.8 jit_solution(11260137274924222153)
XLA Ops:
  0.7 1.0 copy-done.14
  1.6 0.8 copy-done.22
  3.2 2.3 %pack_profiles.1 = (s32[768,128]{1,0:T(8,128)S(1)}, s32[16,512]{1,0:T(8,128)S(1)}, s32[16,512]{1,0:T(8,128)S(1)}) custom-call(bf16[4,4096]{1,0:T(4,128)(2,1)S(1)} %copy-done.22, bf16[16,4096]{1,0:T(8,128)(2,1)S(1)} %copy-done.14, s32[16,512]{1,0:T(8,128)S(1)} %bitcast.25), custom_call_target="tpu_custom_call" | custom-call | tf_op jit(solution)/shard_map/pack_profiles/pallas_call | solution.py:201
  5.5 53.5 %all_to_all.20 = s32[256,1,384]{2,1,0:T(1,128)S(1)} all-to-all(s32[256,1,384]{2,1,0:T(1,128)S(1)} %bitcast.22), channel_id=1, replica_groups=mesh['x'=4,'z'=16,'c'=2,'y'=4] {'x','z','y'}, dimensions={0} | all-to-all | bytes 786432 | tf_op jit(solution)/shard_map/all_to_all | solution.py:596
  59.0 4.6 %collective-permute-start = (s32[768,128]{1,0:T(8,128)S(1)}, s32[768,128]{1,0:T(8,128)S(1)}, u32[]{:S(2)}, u32[]{:S(2)}) collective-permute-start(s32[768,128]{1,0:T(8,128)S(1)} %bitcast.13), channel_id=1, source_target_pairs={{0,4},{4,0},{1,5},{5,1},{2,6},{6,2},{3,7},{7,3},{8,12},{12,8},{9,1... | collective-permute-start | bytes 1179656 | tf_op jit(solution)/shard_map/ppermute | solution.py:598
  63.6 1.3 collective-permute-done.other_ref
  64.9 0.9 copy-done
  65.9 0.9 copy-done.2
  66.8 1.0 copy-done.10
  67.8 1.0 copy-done.11
  68.9 0.9 copy-done.15
  73.6 5.8 %spread.1 = (f32[256,128]{1,0:T(8,128)S(1)}, bf16[4096,256]{1,0:T(8,128)(2,1)S(1)}, f32[256,256]{1,0:T(8,128)S(1)}, s32[32,256]{1,0:T(8,128)S(1)}, s32[32,256]{1,0:T(8,128)S(1)}) custom-call(s32[768,128]{1,0:T(8,128)S(1)} %bitcast.14, s32[768,128]{1,0:T(8,128)S(1)} %collective-permute-done.other_ref, s32[32,256]{1,0:T(8,128)S(1)} %copy-done.24, ...), custom_call_target="tpu_custom_call" | custom-call | tf_op jit(solution)/shard_map/spread/pallas_call | solution.py:359
  79.5 27.3 %all_to_all.21 = f32[256,1,128]{2,1,0:T(1,128)S(1)} all-to-all(f32[256,1,128]{2,1,0:T(1,128)S(1)} %bitcast.24), channel_id=1, replica_groups=mesh['x'=4,'z'=16,'c'=2,'y'=4] {'x','z','y'}, dimensions={0} | all-to-all | bytes 262144 | tf_op jit(solution)/shard_map/all_to_all | solution.py:596
  106.8 3.6 %collective-permute-start.1 = (f32[256,128]{1,0:T(8,128)S(1)}, f32[256,128]{1,0:T(8,128)S(1)}, u32[]{:S(2)}, u32[]{:S(2)}) collective-permute-start(f32[256,128]{1,0:T(8,128)S(1)} %bitcast.18), channel_id=1, source_target_pairs={{0,4},{4,0},{1,5},{5,1},{2,6},{6,2},{3,7},{7,3},{8,12},{12,8},{9,1... | collective-permute-start | bytes 393224 | tf_op jit(solution)/shard_map/ppermute | solution.py:598
  110.4 1.0 collective-permute-done.1.other_ref
  111.4 2.2 %solve_columns.1 = f32[512,128]{1,0:T(8,128)S(1)} custom-call(f32[256,128]{1,0:T(8,128)S(1)} %bitcast.19, f32[256,128]{1,0:T(8,128)S(1)} %collective-permute-done.1.other_ref, bf16[256,64]{1,0:T(8,128)(2,1)S(1)} %copy-done.19, bf16[256,64]{1,0:T(8,128)(2,1)S(1)} %copy-done.18, bf16[64,256]{1,0:T(8,128)(2,1)S(1)} %copy-done.21, ...), custom_call_target="tpu_custom_call" | custom-call | tf_op jit(solution)/shard_map/solve_columns/pallas_call | solution.py:442
  113.7 32.7 %all_to_all.22 = f32[256,1,256]{2,1,0:T(1,128)S(1)} all-to-all(f32[256,1,256]{2,1,0:T(1,128)S(1)} %bitcast.17), channel_id=1, replica_groups=mesh['x'=4,'z'=16,'c'=2,'y'=4] {'x','z','y'}, dimensions={0} | all-to-all | bytes 524288 | tf_op jit(solution)/shard_map/all_to_all | solution.py:596
  146.4 3.5 %collective-permute-start.2 = (f32[512,128]{1,0:T(8,128)S(1)}, f32[512,128]{1,0:T(8,128)S(1)}, u32[]{:S(2)}, u32[]{:S(2)}) collective-permute-start(f32[512,128]{1,0:T(8,128)S(1)} %bitcast.15), channel_id=1, source_target_pairs={{0,4},{4,0},{1,5},{5,1},{2,6},{6,2},{3,7},{7,3},{8,12},{12,8},{9,1... | collective-permute-start | bytes 786440 | tf_op jit(solution)/shard_map/ppermute | solution.py:598
  149.9 1.1 collective-permute-done.2.other_ref
  151.0 4.2 %tile_forces.1 = (bf16[2,8,4096]{2,1,0:T(8,128)(2,1)}, f32[256,128]{1,0:T(8,128)S(1)}) custom-call(f32[512,128]{1,0:T(8,128)S(1)} %bitcast.16, f32[512,128]{1,0:T(8,128)S(1)} %collective-permute-done.2.other_ref, bf16[4096,256]{1,0:T(8,128)(2,1)S(1)} %get-tuple-element.14.wide_ref, f32[256,256]{1,0:T(8,128)S(1)} %get-tuple-element.15.tall_ref, ...), custom_call_target="tpu_custom_call" | custom-call | tf_op jit(solution)/shard_map/tile_forces/pallas_call | solution.py:530
  155.3 27.0 %all_to_all.23 = f32[256,1,128]{2,1,0:T(1,128)S(1)} all-to-all(f32[256,1,128]{2,1,0:T(1,128)S(1)} %bitcast.23), channel_id=1, replica_groups=mesh['x'=4,'z'=16,'c'=2,'y'=4] {'x','z','y'}, dimensions={0} | all-to-all | bytes 262144 | tf_op jit(solution)/shard_map/all_to_all | solution.py:596
  182.3 3.6 %collective-permute-start.3 = (f32[256,128]{1,0:T(8,128)S(1)}, f32[256,128]{1,0:T(8,128)S(1)}, u32[]{:S(2)}, u32[]{:S(2)}) collective-permute-start(f32[256,128]{1,0:T(8,128)S(1)} %bitcast.20), channel_id=1, source_target_pairs={{0,4},{4,0},{1,5},{5,1},{2,6},{6,2},{3,7},{7,3},{8,12},{12,8},{9,1... | collective-permute-start | bytes 393224 | tf_op jit(solution)/shard_map/ppermute | solution.py:598
  185.9 1.0 collective-permute-done.3.other_ref
  186.8 2.0 %gather_forces.1 = f32[2,4096]{1,0:T(2,128)} custom-call(f32[256,128]{1,0:T(8,128)S(1)} %bitcast.21, f32[256,128]{1,0:T(8,128)S(1)} %collective-permute-done.3.other_ref, s32[16,512]{1,0:T(8,128)S(1)} %get-tuple-element.20.low_ref, s32[16,512]{1,0:T(8,128)S(1)} %get-tuple-element.21.high_ref), custom_call_target="tpu_custom_call" | custom-call | tf_op jit(solution)/shard_map/gather_forces/pallas_call | solution.py:580
  (51 shorter events, 4.6 us)
Async XLA Ops:
  0.6 110.7 %copy-start.6 = (bf16[256,1024]{1,0:T(8,128)(2,1)S(1)}, bf16[256,1024]{1,0:T(8,128)(2,1)}, u32[]{:S(2)}) copy-start(bf16[256,1024]{1,0:T(8,128)(2,1)} %constant.55.clone.wave_rest) | copy-start | bytes 1572868
  0.6 110.7 %copy-start.12 = (f32[4,128,128]{2,1,0:T(8,128)S(1)}, f32[4,128,128]{2,1,0:T(8,128)}, u32[]{:S(2)}) copy-start(f32[4,128,128]{2,1,0:T(8,128)} %constant.51.clone.turn_sin) | copy-start | bytes 786436
  0.7 1.0 copy-start.14
  3.1 108.2 %copy-start.18 = (bf16[256,64]{1,0:T(8,128)(2,1)S(1)}, bf16[256,64]{1,0:T(8,128)(2,1)}, u32[]{:S(2)}) copy-start(bf16[256,64]{1,0:T(8,128)(2,1)} %constant.47.clone.first_rest) | copy-start | bytes 98308
  3.1 108.2 %copy-start.19 = (bf16[256,64]{1,0:T(8,128)(2,1)S(1)}, bf16[256,64]{1,0:T(8,128)(2,1)}, u32[]{:S(2)}) copy-start(bf16[256,64]{1,0:T(8,128)(2,1)} %constant.46.clone.first_top) | copy-start | bytes 98308
  3.2 108.2 %copy-start.20 = (bf16[64,256]{1,0:T(8,128)(2,1)S(1)}, bf16[64,256]{1,0:T(8,128)(2,1)}, u32[]{:S(2)}) copy-start(bf16[64,256]{1,0:T(8,128)(2,1)} %constant.49.clone.back_rest) | copy-start | bytes 98308
  3.2 108.2 %copy-start.21 = (bf16[64,256]{1,0:T(8,128)(2,1)S(1)}, bf16[64,256]{1,0:T(8,128)(2,1)}, u32[]{:S(2)}) copy-start(bf16[64,256]{1,0:T(8,128)(2,1)} %constant.48.clone.back_top) | copy-start | bytes 98308
  59.0 5.9 %collective-permute-start = (s32[768,128]{1,0:T(8,128)S(1)}, s32[768,128]{1,0:T(8,128)S(1)}, u32[]{:S(2)}, u32[]{:S(2)}) collective-permute-start(s32[768,128]{1,0:T(8,128)S(1)} %bitcast.13), channel_id=1, source_target_pairs={{0,4},{4,0},{1,5},{5,1},{2,6},{6,2},{3,7},{7,3},{8,12},{12,8},{9,1... | collective-permute-start | bytes 1179656 | tf_op jit(solution)/shard_map/ppermute | solution.py:598
  64.9 0.9 copy-start
  66.8 1.0 copy-start.10
  67.8 1.0 copy-start.11
  73.6 37.8 %copy-start.7 = (bf16[256,1024]{1,0:T(8,128)(2,1)S(1)}, bf16[256,1024]{1,0:T(8,128)(2,1)}, u32[]{:S(2)}) copy-start(bf16[256,1024]{1,0:T(8,128)(2,1)} %constant.54.clone.wave_top) | copy-start | bytes 1572868
  73.6 37.8 %copy-start.8 = (bf16[1024,256]{1,0:T(8,128)(2,1)S(1)}, bf16[1024,256]{1,0:T(8,128)(2,1)}, u32[]{:S(2)}) copy-start(bf16[1024,256]{1,0:T(8,128)(2,1)} %constant.53.clone.second_rest) | copy-start | bytes 1572868
  73.6 37.8 %copy-start.9 = (bf16[1024,256]{1,0:T(8,128)(2,1)S(1)}, bf16[1024,256]{1,0:T(8,128)(2,1)}, u32[]{:S(2)}) copy-start(bf16[1024,256]{1,0:T(8,128)(2,1)} %constant.52.clone.second_top) | copy-start | bytes 1572868
  73.6 37.8 %copy-start.13 = (f32[4,128,128]{2,1,0:T(8,128)S(1)}, f32[4,128,128]{2,1,0:T(8,128)}, u32[]{:S(2)}) copy-start(f32[4,128,128]{2,1,0:T(8,128)} %constant.50.clone.turn_cos) | copy-start | bytes 786436
  79.4 71.6 %copy-start.1 = (f32[128,512]{1,0:T(8,128)S(1)}, f32[128,512]{1,0:T(8,128)}, u32[]{:S(2)}) copy-start(f32[128,512]{1,0:T(8,128)} %constant.43.clone.turn_sin_hbm.turn_sin) | copy-start | bytes 786436
  79.4 71.6 %copy-start.3 = (f32[128,512]{1,0:T(8,128)S(1)}, f32[128,512]{1,0:T(8,128)}, u32[]{:S(2)}) copy-start(f32[128,512]{1,0:T(8,128)} %constant.42.clone.turn_cos_hbm.turn_cos) | copy-start | bytes 786436
  79.4 71.6 %copy-start.4 = (bf16[1024,256]{1,0:T(8,128)(2,1)S(1)}, bf16[1024,256]{1,0:T(8,128)(2,1)}, u32[]{:S(2)}) copy-start(bf16[1024,256]{1,0:T(8,128)(2,1)} %constant.59.clone.last_rest) | copy-start | bytes 1572868
  79.4 71.6 %copy-start.5 = (bf16[1024,256]{1,0:T(8,128)(2,1)S(1)}, bf16[1024,256]{1,0:T(8,128)(2,1)}, u32[]{:S(2)}) copy-start(bf16[1024,256]{1,0:T(8,128)(2,1)} %constant.58.clone.last_top) | copy-start | bytes 1572868
  79.5 71.6 %copy-start.16 = (bf16[256,64]{1,0:T(8,128)(2,1)S(1)}, bf16[256,64]{1,0:T(8,128)(2,1)}, u32[]{:S(2)}) copy-start(bf16[256,64]{1,0:T(8,128)(2,1)} %constant.57.clone.wave_rest) | copy-start | bytes 98308
  79.5 71.6 %copy-start.17 = (bf16[256,64]{1,0:T(8,128)(2,1)S(1)}, bf16[256,64]{1,0:T(8,128)(2,1)}, u32[]{:S(2)}) copy-start(bf16[256,64]{1,0:T(8,128)(2,1)} %constant.56.clone.wave_top) | copy-start | bytes 98308
  106.8 4.6 %collective-permute-start.1 = (f32[256,128]{1,0:T(8,128)S(1)}, f32[256,128]{1,0:T(8,128)S(1)}, u32[]{:S(2)}, u32[]{:S(2)}) collective-permute-start(f32[256,128]{1,0:T(8,128)S(1)} %bitcast.18), channel_id=1, source_target_pairs={{0,4},{4,0},{1,5},{5,1},{2,6},{6,2},{3,7},{7,3},{8,12},{12,8},{9,1... | collective-permute-start | bytes 393224 | tf_op jit(solution)/shard_map/ppermute | solution.py:598
  146.4 4.7 %collective-permute-start.2 = (f32[512,128]{1,0:T(8,128)S(1)}, f32[512,128]{1,0:T(8,128)S(1)}, u32[]{:S(2)}, u32[]{:S(2)}) collective-permute-start(f32[512,128]{1,0:T(8,128)S(1)} %bitcast.15), channel_id=1, source_target_pairs={{0,4},{4,0},{1,5},{5,1},{2,6},{6,2},{3,7},{7,3},{8,12},{12,8},{9,1... | collective-permute-start | bytes 786440 | tf_op jit(solution)/shard_map/ppermute | solution.py:598
  182.3 4.6 %collective-permute-start.3 = (f32[256,128]{1,0:T(8,128)S(1)}, f32[256,128]{1,0:T(8,128)S(1)}, u32[]{:S(2)}, u32[]{:S(2)}) collective-permute-start(f32[256,128]{1,0:T(8,128)S(1)} %bitcast.20), channel_id=1, source_target_pairs={{0,4},{4,0},{1,5},{5,1},{2,6},{6,2},{3,7},{7,3},{8,12},{12,8},{9,1... | collective-permute-start | bytes 393224 | tf_op jit(solution)/shard_map/ppermute | solution.py:598
  (9 other events, 7.2 us)

commit v3 on v2

--- a/solution.py
+++ b/solution.py
@@ -22,6 +22,8 @@
 LOW = 256
 MACRO_LEVEL = 4.0
 SCALE = 8192.0
+OCTAVES = 25.0
+STEPS = 819.0
 SPREAD_GROUP = 16
 FORCE_GROUP = 16
 GATHER_GROUP = 16
@@ -62,24 +64,23 @@
 @functools.cache
 def tables_y():
     lane = np.arange(128)
-    r, c, l = lane // 16, (lane // 8) % 2, lane % 8
+    r, g = lane // 16, lane % 16
     f = np.arange(128)
     a = np.arange(64)
+    a = a % 4 * 16 + a // 4
     turn = np.pi * ((f[:, None] * a[None, :]) % 128) / 64.0
     first = np.concatenate([np.cos(turn), -np.sin(turn)], axis=0)
-    h = np.arange(4)
-    b = 32 * c[None, :] + 8 * h[:, None] + r[None, :]
+    b = 8 * np.arange(8)[:, None] + r[None, :]
     angle = np.pi * (f[None, :, None] * (2 * b[:, None, :] + 1)) / 8192.0
-    w = np.arange(256) // 8
-    l_out = np.arange(256) % 8
-    wave = np.pi * (((2 * b[:, :, None] + 1) * w[None, None, :]) % 128) / 64.0
-    same = l[:, None] == l_out[None, :]
+    w = np.arange(512) // 16
+    wave = np.pi * (((2 * b[:4, :, None] + 1) * w[None, None, :]) % 128) / 64.0
+    same = g[:, None] == (np.arange(512) % 16)[None, :]
     second = np.stack([np.cos(wave) * same[None], np.sin(wave) * same[None]], axis=1)
     return (
         split_host(first),
         np.cos(angle).astype(np.float32),
         np.sin(angle).astype(np.float32),
-        split_host(second.reshape(1024, 256)),
+        split_host(second.reshape(1024, 512)),
     )
 
 
@@ -130,27 +131,49 @@
     return copies
 
 
-def join_cores(own, other, core):
-    lane_core = (lax.broadcasted_iota(I32, own.shape, 1) // 8) % 2
-    moved = jnp.where(core == 0, pltpu.roll(other, 8, 1), pltpu.roll(other, 120, 1))
-    return jnp.where(lane_core == core, own, moved)
+def encode(values):
+    size = jnp.abs(values)
+    level = (jnp.log(jnp.maximum(size, 2.0**-30)) * (1.0 / math.log(2.0)) + OCTAVES) * STEPS
+    level = jnp.clip(jnp.floor(level + 0.5), 0.0, 32767.0).astype(I32)
+    return level + jnp.where(values < 0, 32768, 0)
+
+
+def decode(codes):
+    level = codes & 0x7FFF
+    size = jnp.exp((level.astype(F32) * (1.0 / STEPS) - OCTAVES) * math.log(2.0))
+    size = jnp.where(level == 0, 0.0, size)
+    return jnp.where((codes & 0x8000) != 0, -size, size)
 
 
 def pack_kernel(
-    row_hbm, col_hbm, list_ref, out_ref, low_ref, high_ref, row_ref, col_ref, table, cols, rows, sems
+    row_hbm,
+    col_hbm,
+    list_hbm,
+    out_ref,
+    low_ref,
+    high_ref,
+    row_ref,
+    col_ref,
+    list_ref,
+    table,
+    cols,
+    rows,
+    sems,
 ):
     core = lax.axis_index("c")
-    copies = load_all([(col_hbm, col_ref), (row_hbm, row_ref)], sems)
+    copies = load_all([(list_hbm, list_ref), (col_hbm, col_ref), (row_hbm, row_ref)], sems)
+    copies[0].wait()
     listed = list_ref[...].astype(F32)
     empty = listed >= CELL_DEV
     high = jnp.floor(listed * (1.0 / LOW))
     low = jnp.where(empty, float(LOW), listed - high * LOW)
     target = lax.broadcasted_iota(I32, (512, 512), 1)
-    source = (target % 256) // 4 * 8 + ((target // 256) ^ core) * 4 + target % 4
+    chip = target // 4 % 4 * 16 + target // 16 % 16
+    source = chip * 8 + ((target // 256) ^ core) * 4 + target % 4
     move = jnp.where(lax.broadcasted_iota(I32, (512, 512), 0) == source, 1.0, 0.0).astype(BF16)
     high_ref[...] = dot(high.astype(BF16), move).astype(I32)
     low_ref[...] = dot(low.astype(BF16), move).astype(I32)
-    for copy in copies:
+    for copy in copies[1:]:
         copy.wait()
     for h in range(16):
         table[h * 16 : h * 16 + 16, :] = col_ref[:, h * LOW : (h + 1) * LOW]
@@ -205,23 +228,26 @@
             jax.ShapeDtypeStruct((16, 512), I32),
             jax.ShapeDtypeStruct((16, 512), I32),
         ),
-        in_specs=[HBM, HBM, VMEM],
+        in_specs=[HBM, HBM, HBM],
         scratch_shapes=[
             pltpu.VMEM((BH, CELL_DEV), BF16),
             pltpu.VMEM((BW, CELL_DEV), BF16),
+            pltpu.VMEM((CAP, 512), I32),
             pltpu.VMEM((320, 256), BF16),
             pltpu.VMEM((128, 512), I32),
             pltpu.VMEM((32, 512), I32),
-            pltpu.SemaphoreType.DMA((2,)),
+            pltpu.SemaphoreType.DMA((3,)),
         ],
-        compiler_params=pltpu.CompilerParams(vmem_limit_bytes=32 << 20),
+        compiler_params=pltpu.CompilerParams(vmem_limit_bytes=60 << 20),
+        cost_estimate=pl.CostEstimate(flops=15000000000, bytes_accessed=10000000, transcendentals=0),
         name="pack_profiles",
     )(row_profile, col_profile, send_list.T)
 
 
 def slot_address(slots, core):
     source = slots // 16
-    low = source // 8 * 4 + source % 4
+    low = source // 8 % 16 * 16 + source // 128 * 4 + source % 4
+    low = jnp.where(source < 512, low, LOW)
     high = (((source // 4) % 2) ^ core) * 16 + slots % 16
     return low, high
 
@@ -373,40 +399,56 @@
             pltpu.SemaphoreType.DMA((len(loaded),)),
         ],
         compiler_params=pltpu.CompilerParams(vmem_limit_bytes=40 << 20),
+        cost_estimate=pl.CostEstimate(flops=60000000000, bytes_accessed=30000000, transcendentals=0),
         name="spread",
     )(own, other, *loaded)
+
+
+def column_kernel(
+    got_ref, first_top, first_rest, turn_cos, turn_sin, second_top, second_rest, out_ref
+):
+    core = lax.axis_index("c")
+    first = (first_top[...], first_rest[...])
+    parts = []
+    for h in range(4):
+        mixed = dot3(first, halves(got_ref[pl.ds(h, 64, stride=4), :]))
+        real, imag = mixed[:128], mixed[128:]
+        cos, sin = turn_cos[core * 4 + h], turn_sin[core * 4 + h]
+        parts += [real * cos + imag * sin, imag * cos - real * sin]
+    partial = dot3(halves(jnp.concatenate(parts, axis=1)), (second_top[...], second_rest[...]))
+    odd = (lax.broadcasted_iota(I32, (128, 512), 1) // 16) % 2
+    out_ref[...] = jnp.where(odd * core == 1, -partial, partial)
+
+
+def transform_columns(got):
+    first, cos, sin, second = tables_y()
+    return pl.pallas_call(
+        column_kernel,
+        out_shape=jax.ShapeDtypeStruct((128, 512), F32),
+        compiler_params=pltpu.CompilerParams(vmem_limit_bytes=32 << 20),
+        cost_estimate=pl.CostEstimate(
+            flops=20000000000, bytes_accessed=20000000, transcendentals=0
+        ),
+        name="transform_columns",
+    )(got, *first, cos, sin, *second)
 
 
 def solve_kernel(
     own_ref,
     other_ref,
-    first_top,
-    first_rest,
     back_top,
     back_rest,
     turn_cos,
     turn_sin,
-    second_top,
-    second_rest,
     wave_top,
     wave_rest,
     out_ref,
-    held,
 ):
     core = lax.axis_index("c")
-    place = (lax.axis_index("x") * 16 + lax.axis_index("z")) * 4 + lax.axis_index("y")
-    held[...] = join_cores(own_ref[...], other_ref[...], core)
-    first = (first_top[...], first_rest[...])
-    parts = []
-    for h in range(4):
-        mixed = dot3(first, halves(held[pl.ds(h, 64, stride=4), :]))
-        real, imag = mixed[:128], mixed[128:]
-        cos, sin = turn_cos[h], turn_sin[h]
-        parts += [real * cos + imag * sin, imag * cos - real * sin]
-    spectrum = dot3(halves(jnp.concatenate(parts, axis=1)), (second_top[...], second_rest[...]))
-    lane = lax.broadcasted_iota(I32, (128, 256), 1)
-    wave_u = lax.broadcasted_iota(I32, (128, 256), 0) + 128 * (lane // 8)
-    wave_v = (place // 64) * 16 + core * 8 + lane % 8 + 64 * (place % 64)
+    place = (lax.axis_index("z") * 4 + lax.axis_index("x")) * 4 + lax.axis_index("y")
+    lane = lax.broadcasted_iota(I32, (128, 512), 1)
+    wave_u = lax.broadcasted_iota(I32, (128, 512), 0) + 128 * (lane // 16)
+    wave_v = (place // 64) * 16 + lane % 16 + 64 * (place % 64)
     freq_u = wave_u.astype(F32) * (math.pi / GRID)
     freq_v = wave_v.astype(F32) * (math.pi / GRID)
     radius = freq_u * freq_u + freq_v * freq_v
@@ -415,12 +457,13 @@
     kernel = jnp.where(
         radius > 0, weight_u * weight_v / jnp.where(radius > 0, radius, 1.0), 0.0
     )
-    scaled = spectrum * kernel
+    kernel = jnp.where((lane // 16) % 2 * core == 1, -kernel, kernel)
+    scaled = (own_ref[...] + other_ref[...]) * kernel
     both = jnp.concatenate([scaled * freq_v, scaled * freq_u], axis=0)
     waves = dot3(halves(both), (wave_top[...], wave_rest[...]))
     back = (back_top[...], back_rest[...])
     for h in range(4):
-        cos, sin = turn_cos[h], turn_sin[h]
+        cos, sin = turn_cos[core * 4 + h], turn_sin[core * 4 + h]
         maps = []
         for m in range(2):
             rows = slice(m * 128, m * 128 + 128)
@@ -430,9 +473,8 @@
             out_imag = real * sin + imag * cos
             pair = [out_real, out_imag] if m == 0 else [out_imag, -out_real]
             maps.append(jnp.concatenate(pair, axis=0))
-        result = dot3(back, halves(jnp.concatenate(maps, axis=1)))
-        for m in range(2):
-            out_ref[pl.ds(2 * h + m, 64, stride=8), :] = result[:, m * 128 : m * 128 + 128]
+        codes = encode(dot3(back, halves(jnp.concatenate(maps, axis=1))))
+        out_ref[pl.ds(h, 64, stride=4), :] = codes[:, :128] + (codes[:, 128:] << 16)
 
 
 def solve_columns(own, other):
@@ -441,16 +483,17 @@
     wave = tuple(np.ascontiguousarray(part.T) for part in second)
     return pl.pallas_call(
         solve_kernel,
-        out_shape=jax.ShapeDtypeStruct((512, 128), F32),
-        scratch_shapes=[pltpu.VMEM((256, 128), F32)],
-        compiler_params=pltpu.CompilerParams(vmem_limit_bytes=40 << 20),
+        out_shape=jax.ShapeDtypeStruct((256, 128), I32),
+        compiler_params=pltpu.CompilerParams(vmem_limit_bytes=32 << 20),
+        cost_estimate=pl.CostEstimate(
+            flops=20000000000, bytes_accessed=20000000, transcendentals=0
+        ),
         name="solve_columns",
-    )(own, other, *first, *back, cos, sin, *second, *wave)
+    )(own, other, *back, cos, sin, *wave)
 
 
 def force_kernel(
-    own_ref,
-    other_ref,
+    got_ref,
     wide_ref,
     tall_ref,
     low_ref,
@@ -463,15 +506,12 @@
     last_rest,
     fields_ref,
     out_ref,
-    held,
     field,
     total,
 ):
-    core = lax.axis_index("c")
-    held[...] = join_cores(own_ref[...], other_ref[...], core)
-    columns = [
-        held[pl.ds(q * 128 + m, 64, stride=2), :] for m in range(2) for q in range(4)
-    ]
+    codes = got_ref[...]
+    maps = [decode(codes), decode(codes >> 16)]
+    columns = [maps[m][q * 64 : q * 64 + 64] for m in range(2) for q in range(4)]
     waves = dot3((wave_top[...], wave_rest[...]), halves(jnp.concatenate(columns, axis=1)))
     cos, sin = turn_cos[...], turn_sin[...]
     maps = []
@@ -523,7 +563,7 @@
     out_ref[...] = jnp.concatenate([summed, summed], axis=0).T
 
 
-def tile_forces(own, other, wide, tall, low, high):
+def tile_forces(got, wide, tall, low, high):
     last, cos, sin, wave = tables_x()
     last = tuple(np.ascontiguousarray(part.T) for part in last)
     wave = tuple(np.ascontiguousarray(part.T) for part in wave)
@@ -534,13 +574,13 @@
             jax.ShapeDtypeStruct((256, 128), F32),
         ),
         scratch_shapes=[
-            pltpu.VMEM((512, 128), F32),
             pltpu.VMEM((256, 256), F32),
             pltpu.VMEM((128, 256), F32),
         ],
         compiler_params=pltpu.CompilerParams(vmem_limit_bytes=40 << 20),
+        cost_estimate=pl.CostEstimate(flops=40000000000, bytes_accessed=30000000, transcendentals=0),
         name="tile_forces",
-    )(own, other, wide, tall, low, high, *wave, cos, sin, *last)
+    )(got, wide, tall, low, high, *wave, cos, sin, *last)
 
 
 def gather_kernel(own_ref, other_ref, low_ref, high_ref, out_ref, own, other, total):
@@ -586,27 +626,32 @@
             pltpu.VMEM((64, 256), F32),
         ],
         compiler_params=pltpu.CompilerParams(vmem_limit_bytes=32 << 20),
+        cost_estimate=pl.CostEstimate(flops=20000000000, bytes_accessed=5000000, transcendentals=0),
         name="gather_forces",
     )(own, other, low, high)
 
 
-def exchange(words):
+def between_chips(words):
     rows = words.shape[0]
     sent = words.reshape(256, 1, rows // 256 * 128)
-    own = lax.all_to_all(sent, ("x", "z", "y"), split_axis=0, concat_axis=0, tiled=True)
-    own = own.reshape(rows, 128)
+    got = lax.all_to_all(sent, ("z", "x", "y"), split_axis=0, concat_axis=0, tiled=True)
+    return got.reshape(rows, 128)
+
+
+def with_other(own):
     return own, lax.ppermute(own, "c", [(0, 1), (1, 0)])
 
 
 def per_device(row_profile, col_profile, send_list, tile_list, row_offset, col_offset, macro_mask):
     words, cell_low, cell_high = pack_profiles(row_profile, col_profile, send_list)
-    own, other = exchange(words)
+    own, other = with_other(between_chips(words))
     lines, wide, tall, slot_low, slot_high = spread(
         own, other, tile_list, row_offset, col_offset, macro_mask
     )
-    maps = solve_columns(*exchange(lines))
-    fields, forces = tile_forces(*exchange(maps), wide, tall, slot_low, slot_high)
-    cell_force = gather_forces(*exchange(forces), cell_low, cell_high)
+    partial = transform_columns(between_chips(lines))
+    maps = solve_columns(*with_other(partial))
+    fields, forces = tile_forces(between_chips(maps), wide, tall, slot_low, slot_high)
+    cell_force = gather_forces(*with_other(between_chips(forces)), cell_low, cell_high)
     return (fields, cell_force)
 
 

time: 190 us -> 164 us (0.86)
  blocking collectives: 140 us -> 125 us
  local copies, waits for them, and re-layouts: 11.2 us -> 0.15 us
    all_to_all x4, blocking collectives: 140 us -> 125 us  [between_chips(): lax.all_to_all(sent, ('z', 'x', 'y'), split_axis=0, concat_axis=0, tiled=...]
    unnamed x58 -> x52, local copies, waits for them, and re-layouts: 11.2 us -> 0.15 us
    ppermute x4 -> x3, starting transfers between devices: 15.2 us -> 16.4 us  [with_other(): return (own, lax.ppermute(own, 'c', [(0, 1), (1, 0)]))]
    ppermute x4 -> x3, waiting for transfers between devices: 4.4 us -> 3.43 us  [with_other(): return (own, lax.ppermute(own, 'c', [(0, 1), (1, 0)]))]
  transfers between devices with their start and end apart: 4 -> 3, of which waited for: 4 -> 3; matrix products, arithmetic and copies ran while one was open for 0% -> 0% of each run, Pallas kernels for 0% -> 0%
where the time goes in v3:
time: 164 us
  blocking collectives  125 us (76%)
  Pallas kernels  18.1 us (11%)
  starting transfers between devices  16.4 us (10%)
  waiting for transfers between devices  3.43 us (2%)
    all_to_all x4, blocking collectives, between_chips(): lax.all_to_all(sent, ('z', 'x', 'y'), split_axis=0, concat_axis=0, tiled=...  125 us
    ppermute x3, starting transfers between devices, with_other(): return (own, lax.ppermute(own, 'c', [(0, 1), (1, 0)]))  16.4 us
    pallas_call x1, Pallas kernels, spread(): pl.pallas_call(spread_kernel, out_shape=(jax.ShapeDtypeStruct((256, 128),...  5.84 us
    pallas_call x1, Pallas kernels, tile_forces(): pl.pallas_call(force_kernel, out_shape=(jax.ShapeDtypeStruct((2, TH, GRID...  4.11 us
    pallas_call x1, Pallas kernels, pack_profiles(): pl.pallas_call(pack_kernel, out_shape=(jax.ShapeDtypeStruct((768, 128), I...  3.79 us
    ppermute x3, waiting for transfers between devices, with_other(): return (own, lax.ppermute(own, 'c', [(0, 1), (1, 0)]))  3.43 us
  transfers between devices with their start and end apart: 3, of which 3 were waited for; matrix products, arithmetic and copies ran while one was open for 0% of the time, Pallas kernels for 0%

profile of v3, /device:TPU:1, one launch (start us, length us, event | category | flops | bytes accessed | tf_op | source)
XLA Modules:
  0.0 164.0 jit_solution(11007507120105589074)
XLA Ops:
  0.7 0.0 copy-start.13
  0.7 0.0 copy-start.14
  0.7 0.0 copy-start.15
  0.7 0.0 copy-start.22
  0.7 0.0 copy-start.23
  0.7 3.8 %pack_profiles.1 = (s32[768,128]{1,0:T(8,128)}, s32[16,512]{1,0:T(8,128)}, s32[16,512]{1,0:T(8,128)}) custom-call(bf16[4,4096]{1,0:T(4,128)(2,1)} %row_hbm.2, bf16[16,4096]{1,0:T(8,128)(2,1)} %col_hbm.2, s32[16,512]{1,0:T(8,128)} %bitcast.25), custom_call_target="tpu_custom_call" | custom-call | flops 15000000512 | bytes 10000000 | tf_op jit(solution)/shard_map/pack_profiles/pallas_call | solution.py:224
  4.5 51.0 %all_to_all.20 = s32[256,1,384]{2,1,0:T(1,128)S(1)} all-to-all(s32[256,1,384]{2,1,0:T(1,128)} %bitcast.24), channel_id=1, replica_groups=mesh['x'=4,'z'=16,'c'=2,'y'=4] {'z','x','y'}, dimensions={0} | all-to-all | bytes 786432 | tf_op jit(solution)/shard_map/all_to_all | solution.py:637
  55.6 0.0 copy-start.18
  55.6 0.0 copy-start.19
  55.6 5.5 %collective-permute-start = (s32[768,128]{1,0:T(8,128)S(1)}, s32[768,128]{1,0:T(8,128)S(1)}, u32[]{:S(2)}, u32[]{:S(2)}) collective-permute-start(s32[768,128]{1,0:T(8,128)S(1)} %bitcast.15), channel_id=1, source_target_pairs={{0,4},{4,0},{1,5},{5,1},{2,6},{6,2},{3,7},{7,3},{8,12},{12,8},{9,1... | collective-permute-start | bytes 1179656 | tf_op jit(solution)/shard_map/ppermute | solution.py:642
  61.1 1.3 collective-permute-done.other_ref
  62.5 5.8 %spread.1 = (f32[256,128]{1,0:T(8,128)S(1)}, bf16[4096,256]{1,0:T(8,128)(2,1)S(1)}, f32[256,256]{1,0:T(8,128)S(1)}, s32[32,256]{1,0:T(8,128)S(1)}, s32[32,256]{1,0:T(8,128)S(1)}) custom-call(s32[768,128]{1,0:T(8,128)S(1)} %bitcast.16, s32[768,128]{1,0:T(8,128)S(1)} %collective-permute-done.other_ref, s32[32,256]{1,0:T(8,128)S(1)} %copy-done.1, ...), custom_call_target="tpu_custom_call" | custom-call | flops 60000002048 | bytes 30000000 | tf_op jit(solution)/shard_map/spread/pallas_call | solution.py:385
  68.4 24.4 %all_to_all.21 = f32[256,1,128]{2,1,0:T(1,128)S(1)} all-to-all(f32[256,1,128]{2,1,0:T(1,128)S(1)} %bitcast.19), channel_id=1, replica_groups=mesh['x'=4,'z'=16,'c'=2,'y'=4] {'z','x','y'}, dimensions={0} | all-to-all | bytes 262144 | tf_op jit(solution)/shard_map/all_to_all | solution.py:637
  92.9 0.0 copy-start.4
  92.9 0.8 transform_columns.1.own_ref
  93.8 5.3 %collective-permute-start.1 = (f32[128,512]{1,0:T(8,128)S(1)}, f32[128,512]{1,0:T(8,128)S(1)}, u32[]{:S(2)}, u32[]{:S(2)}) collective-permute-start(f32[128,512]{1,0:T(8,128)S(1)} %transform_columns.1.own_ref), channel_id=1, source_target_pairs={{0,4},{4,0},{1,5},{5,1},{2,6},{6,2},{3,7},{7,3},{8,12},{12,8},{9,1... | collective-permute-start | bytes 786440 | tf_op jit(solution)/shard_map/ppermute | solution.py:642
  99.2 1.1 collective-permute-done.1.other_ref
  100.3 1.5 solve_columns.1
  101.8 24.5 %all_to_all.22 = s32[256,1,128]{2,1,0:T(1,128)S(1)} all-to-all(s32[256,1,128]{2,1,0:T(1,128)S(1)} %bitcast.22), channel_id=1, replica_groups=mesh['x'=4,'z'=16,'c'=2,'y'=4] {'z','x','y'}, dimensions={0} | all-to-all | bytes 262144 | tf_op jit(solution)/shard_map/all_to_all | solution.py:637
  126.4 4.1 %tile_forces.1 = (bf16[2,8,4096]{2,1,0:T(8,128)(2,1)}, f32[256,128]{1,0:T(8,128)S(1)}) custom-call(s32[256,128]{1,0:T(8,128)S(1)} %bitcast.17, bf16[4096,256]{1,0:T(8,128)(2,1)S(1)} %get-tuple-element.14.wide_ref, f32[256,256]{1,0:T(8,128)S(1)} %get-tuple-element.15.tall_ref, s32[32,256]{1,0:T(8,128)S(1)} %get-tuple-element.16.low_ref, ...), custom_call_target="tpu_custom_call" | custom-call | flops 40000000000 | bytes 30000000 | tf_op jit(solution)/shard_map/tile_forces/pallas_call | solution.py:570
  130.5 25.0 %all_to_all.23 = f32[256,1,128]{2,1,0:T(1,128)S(1)} all-to-all(f32[256,1,128]{2,1,0:T(1,128)S(1)} %bitcast.18), channel_id=1, replica_groups=mesh['x'=4,'z'=16,'c'=2,'y'=4] {'z','x','y'}, dimensions={0} | all-to-all | bytes 262144 | tf_op jit(solution)/shard_map/all_to_all | solution.py:637
  155.5 5.6 %collective-permute-start.2 = (f32[256,128]{1,0:T(8,128)S(1)}, f32[256,128]{1,0:T(8,128)S(1)}, u32[]{:S(2)}, u32[]{:S(2)}) collective-permute-start(f32[256,128]{1,0:T(8,128)S(1)} %bitcast.20), channel_id=1, source_target_pairs={{0,4},{4,0},{1,5},{5,1},{2,6},{6,2},{3,7},{7,3},{8,12},{12,8},{9,1... | collective-permute-start | bytes 393224 | tf_op jit(solution)/shard_map/ppermute | solution.py:642
  161.1 1.0 collective-permute-done.2.other_ref
  162.0 2.0 %gather_forces.1 = f32[2,4096]{1,0:T(2,128)} custom-call(f32[256,128]{1,0:T(8,128)S(1)} %bitcast.21, f32[256,128]{1,0:T(8,128)S(1)} %collective-permute-done.2.other_ref, s32[16,512]{1,0:T(8,128)S(1)} %copy-done.24, s32[16,512]{1,0:T(8,128)S(1)} %copy-done.25), custom_call_target="tpu_custom_call" | custom-call | flops 20000000000 | bytes 5000000 | tf_op jit(solution)/shard_map/gather_forces/pallas_call | solution.py:620
  (44 shorter events, 0.1 us)
Async XLA Ops:
  0.6 61.8 %copy-start = (s32[8,4096]{1,0:T(8,128)S(1)}, s32[8,4096]{1,0:T(8,128)}, u32[]{:S(2)}) copy-start(s32[8,4096]{1,0:T(8,128)} %mask_hbm.1) | copy-start | bytes 393220
  0.6 61.8 %copy-start.1 = (s32[32,256]{1,0:T(8,128)S(1)}, s32[32,256]{1,0:T(8,128)}, u32[]{:S(2)}) copy-start(s32[32,256]{1,0:T(8,128)} %list_hbm.1) | copy-start | bytes 98308
  0.7 61.8 %copy-start.2 = (s32[32,256]{1,0:T(8,128)S(1)}, s32[32,256]{1,0:T(8,128)}, u32[]{:S(2)}) copy-start(s32[32,256]{1,0:T(8,128)} %row_hbm.3) | copy-start | bytes 98308
  0.7 61.8 %copy-start.3 = (s32[32,256]{1,0:T(8,128)S(1)}, s32[32,256]{1,0:T(8,128)}, u32[]{:S(2)}) copy-start(s32[32,256]{1,0:T(8,128)} %col_hbm.3) | copy-start | bytes 98308
  0.7 61.8 %copy-start.12 = (bf16[256,1024]{1,0:T(8,128)(2,1)S(1)}, bf16[256,1024]{1,0:T(8,128)(2,1)}, u32[]{:S(2)}) copy-start(bf16[256,1024]{1,0:T(8,128)(2,1)} %constant.41.clone.first_rest_hbm) | copy-start | bytes 1572868
  0.7 61.8 %copy-start.13 = (bf16[256,1024]{1,0:T(8,128)(2,1)S(1)}, bf16[256,1024]{1,0:T(8,128)(2,1)}, u32[]{:S(2)}) copy-start(bf16[256,1024]{1,0:T(8,128)(2,1)} %constant.40.clone.first_top_hbm) | copy-start | bytes 1572868
  0.7 61.8 %copy-start.14 = (f32[128,512]{1,0:T(8,128)S(1)}, f32[128,512]{1,0:T(8,128)}, u32[]{:S(2)}) copy-start(f32[128,512]{1,0:T(8,128)} %constant.43.clone.turn_sin_hbm.turn_sin) | copy-start | bytes 786436
  0.7 61.8 %copy-start.15 = (f32[128,512]{1,0:T(8,128)S(1)}, f32[128,512]{1,0:T(8,128)}, u32[]{:S(2)}) copy-start(f32[128,512]{1,0:T(8,128)} %constant.42.clone.turn_cos_hbm.turn_cos) | copy-start | bytes 786436
  0.7 61.8 %copy-start.22 = (bf16[64,256]{1,0:T(8,128)(2,1)S(1)}, bf16[64,256]{1,0:T(8,128)(2,1)}, u32[]{:S(2)}) copy-start(bf16[64,256]{1,0:T(8,128)(2,1)} %constant.45.clone.second_rest_hbm) | copy-start | bytes 98308
  0.7 61.8 %copy-start.23 = (bf16[64,256]{1,0:T(8,128)(2,1)S(1)}, bf16[64,256]{1,0:T(8,128)(2,1)}, u32[]{:S(2)}) copy-start(bf16[64,256]{1,0:T(8,128)(2,1)} %constant.44.clone.second_top_hbm) | copy-start | bytes 98308
  55.6 37.3 %copy-start.6 = (bf16[1024,512]{1,0:T(8,128)(2,1)S(1)}, bf16[1024,512]{1,0:T(8,128)(2,1)}, u32[]{:S(2)}) copy-start(bf16[1024,512]{1,0:T(8,128)(2,1)} %constant.51.clone.second_rest) | copy-start | bytes 3145732
  55.6 37.3 %copy-start.7 = (bf16[1024,512]{1,0:T(8,128)(2,1)S(1)}, bf16[1024,512]{1,0:T(8,128)(2,1)}, u32[]{:S(2)}) copy-start(bf16[1024,512]{1,0:T(8,128)(2,1)} %constant.50.clone.second_top) | copy-start | bytes 3145732
  55.6 37.3 %copy-start.10 = (f32[8,128,128]{2,1,0:T(8,128)S(1)}, f32[8,128,128]{2,1,0:T(8,128)}, u32[]{:S(2)}) copy-start(f32[8,128,128]{2,1,0:T(8,128)} %constant.49.clone.turn_sin) | copy-start | bytes 1572868
  55.6 37.3 %copy-start.11 = (f32[8,128,128]{2,1,0:T(8,128)S(1)}, f32[8,128,128]{2,1,0:T(8,128)}, u32[]{:S(2)}) copy-start(f32[8,128,128]{2,1,0:T(8,128)} %constant.48.clone.turn_cos) | copy-start | bytes 1572868
  55.6 37.3 %copy-start.18 = (bf16[256,64]{1,0:T(8,128)(2,1)S(1)}, bf16[256,64]{1,0:T(8,128)(2,1)}, u32[]{:S(2)}) copy-start(bf16[256,64]{1,0:T(8,128)(2,1)} %constant.47.clone.first_rest) | copy-start | bytes 98308
  55.6 37.3 %copy-start.19 = (bf16[256,64]{1,0:T(8,128)(2,1)S(1)}, bf16[256,64]{1,0:T(8,128)(2,1)}, u32[]{:S(2)}) copy-start(bf16[256,64]{1,0:T(8,128)(2,1)} %constant.46.clone.first_top) | copy-start | bytes 98308
  55.6 6.8 %collective-permute-start = (s32[768,128]{1,0:T(8,128)S(1)}, s32[768,128]{1,0:T(8,128)S(1)}, u32[]{:S(2)}, u32[]{:S(2)}) collective-permute-start(s32[768,128]{1,0:T(8,128)S(1)} %bitcast.15), channel_id=1, source_target_pairs={{0,4},{4,0},{1,5},{5,1},{2,6},{6,2},{3,7},{7,3},{8,12},{12,8},{9,1... | collective-permute-start | bytes 1179656 | tf_op jit(solution)/shard_map/ppermute | solution.py:642
  93.8 32.6 %copy-start.8 = (bf16[1024,256]{1,0:T(8,128)(2,1)S(1)}, bf16[1024,256]{1,0:T(8,128)(2,1)}, u32[]{:S(2)}) copy-start(bf16[1024,256]{1,0:T(8,128)(2,1)} %constant.59.clone.last_rest) | copy-start | bytes 1572868
  93.8 32.5 %copy-start.9 = (bf16[1024,256]{1,0:T(8,128)(2,1)S(1)}, bf16[1024,256]{1,0:T(8,128)(2,1)}, u32[]{:S(2)}) copy-start(bf16[1024,256]{1,0:T(8,128)(2,1)} %constant.58.clone.last_top) | copy-start | bytes 1572868
  93.8 32.5 %copy-start.16 = (bf16[256,64]{1,0:T(8,128)(2,1)S(1)}, bf16[256,64]{1,0:T(8,128)(2,1)}, u32[]{:S(2)}) copy-start(bf16[256,64]{1,0:T(8,128)(2,1)} %constant.57.clone.wave_rest) | copy-start | bytes 98308
  93.8 6.5 %collective-permute-start.1 = (f32[128,512]{1,0:T(8,128)S(1)}, f32[128,512]{1,0:T(8,128)S(1)}, u32[]{:S(2)}, u32[]{:S(2)}) collective-permute-start(f32[128,512]{1,0:T(8,128)S(1)} %transform_columns.1.own_ref), channel_id=1, source_target_pairs={{0,4},{4,0},{1,5},{5,1},{2,6},{6,2},{3,7},{7,3},{8,12},{12,8},{9,1... | collective-permute-start | bytes 786440 | tf_op jit(solution)/shard_map/ppermute | solution.py:642
  126.3 35.7 %copy-start.24 = (s32[16,512]{1,0:T(8,128)S(1)}, s32[16,512]{1,0:T(8,128)}, u32[]{:S(2)}) copy-start(s32[16,512]{1,0:T(8,128)} %get-tuple-element.20.low_ref) | copy-start | bytes 98308
  126.3 35.7 %copy-start.25 = (s32[16,512]{1,0:T(8,128)S(1)}, s32[16,512]{1,0:T(8,128)}, u32[]{:S(2)}) copy-start(s32[16,512]{1,0:T(8,128)} %get-tuple-element.21.high_ref) | copy-start | bytes 98308
  155.5 6.5 %collective-permute-start.2 = (f32[256,128]{1,0:T(8,128)S(1)}, f32[256,128]{1,0:T(8,128)S(1)}, u32[]{:S(2)}, u32[]{:S(2)}) collective-permute-start(f32[256,128]{1,0:T(8,128)S(1)} %bitcast.20), channel_id=1, source_target_pairs={{0,4},{4,0},{1,5},{5,1},{2,6},{6,2},{3,7},{7,3},{8,12},{12,8},{9,1... | collective-permute-start | bytes 393224 | tf_op jit(solution)/shard_map/ppermute | solution.py:642
  (5 other events, 62.2 us)

commit v4 on v3

--- a/solution.py
+++ b/solution.py
@@ -24,12 +24,19 @@
 SCALE = 8192.0
 OCTAVES = 25.0
 STEPS = 819.0
-SPREAD_GROUP = 16
+SPREAD_GROUP = 32
 FORCE_GROUP = 16
 GATHER_GROUP = 16
 F32 = jnp.float32
 BF16 = jnp.bfloat16
 I32 = jnp.int32
+
+AXES = ("x", "z3", "z2", "z1", "z0", "c", "y")
+CHIPS = ("z0", "z1", "z2", "z3", "x", "y")
+
+
+def turned(z):
+    return (z & 1) * 8 + (z & 2) * 2 + (z & 4) // 2 + (z & 8) // 8
 
 
 def split_host(values):
@@ -67,7 +74,7 @@
     r, g = lane // 16, lane % 16
     f = np.arange(128)
     a = np.arange(64)
-    a = a % 4 * 16 + a // 4
+    a = a % 4 * 16 + turned(a // 4)
     turn = np.pi * ((f[:, None] * a[None, :]) % 128) / 64.0
     first = np.concatenate([np.cos(turn), -np.sin(turn)], axis=0)
     b = 8 * np.arange(8)[:, None] + r[None, :]
@@ -162,15 +169,16 @@
 ):
     core = lax.axis_index("c")
     copies = load_all([(list_hbm, list_ref), (col_hbm, col_ref), (row_hbm, row_ref)], sems)
+    target = lax.broadcasted_iota(I32, (1, 512), 1)
+    chip = target // 4 % 4 * 16 + turned(target // 16 % 16)
+    source = chip * 8 + ((target // 256) ^ core) * 4 + target % 4
+    lines = lax.broadcasted_iota(I32, (512, 512), 0)
+    move = jnp.where(lines == source, 1.0, 0.0).astype(BF16)
     copies[0].wait()
     listed = list_ref[...].astype(F32)
     empty = listed >= CELL_DEV
     high = jnp.floor(listed * (1.0 / LOW))
     low = jnp.where(empty, float(LOW), listed - high * LOW)
-    target = lax.broadcasted_iota(I32, (512, 512), 1)
-    chip = target // 4 % 4 * 16 + target // 16 % 16
-    source = chip * 8 + ((target // 256) ^ core) * 4 + target % 4
-    move = jnp.where(lax.broadcasted_iota(I32, (512, 512), 0) == source, 1.0, 0.0).astype(BF16)
     high_ref[...] = dot(high.astype(BF16), move).astype(I32)
     low_ref[...] = dot(low.astype(BF16), move).astype(I32)
     for copy in copies[1:]:
@@ -246,7 +254,7 @@
 
 def slot_address(slots, core):
     source = slots // 16
-    low = source // 8 % 16 * 16 + source // 128 * 4 + source % 4
+    low = turned(source // 8) * 16 + source // 128 * 4 + source % 4
     low = jnp.where(source < 512, low, LOW)
     high = (((source // 4) % 2) ^ core) * 16 + slots % 16
     return low, high
@@ -255,21 +263,6 @@
 def spread_kernel(
     own_ref,
     other_ref,
-    list_hbm,
-    row_hbm,
-    col_hbm,
-    mask_hbm,
-    first_top_hbm,
-    first_rest_hbm,
-    turn_cos_hbm,
-    turn_sin_hbm,
-    second_top_hbm,
-    second_rest_hbm,
-    out_ref,
-    wide_ref,
-    tall_ref,
-    low_ref,
-    high_ref,
     list_ref,
     row_ref,
     col_ref,
@@ -280,26 +273,15 @@
     turn_sin,
     second_top,
     second_rest,
+    out_ref,
+    wide_ref,
+    tall_ref,
+    low_ref,
+    high_ref,
     table,
     density,
-    sems,
 ):
     core = lax.axis_index("c")
-    copies = load_all(
-        [
-            (list_hbm, list_ref),
-            (row_hbm, row_ref),
-            (col_hbm, col_ref),
-            (mask_hbm, mask_ref),
-            (first_top_hbm, first_top),
-            (first_rest_hbm, first_rest),
-            (turn_cos_hbm, turn_cos),
-            (turn_sin_hbm, turn_sin),
-            (second_top_hbm, second_top),
-            (second_rest_hbm, second_rest),
-        ],
-        sems,
-    )
     for s, ref in enumerate((own_ref, other_ref)):
         words = ref[pl.ds(s, 256, stride=3), :].T
         for part, piece in enumerate((words & 0xFFFF, words >> 16)):
@@ -311,8 +293,6 @@
     for part, piece in enumerate((words & 0xFFFF, words >> 16)):
         start = 512 + part * 64
         table[start : start + 64, :] = (piece.astype(F32) * (1.0 / SCALE)).astype(BF16)
-    for copy in copies[:4]:
-        copy.wait()
     low, high = slot_address(list_ref[...], core)
     low_ref[...] = low
     high_ref[...] = high
@@ -367,10 +347,7 @@
         return carry
 
     lax.fori_loop(0, NT // SPREAD_GROUP, step, 0)
-    for copy in copies[4:]:
-        copy.wait()
-    turned = halves(density[...].T)
-    mixed = dot3(turned, (first_top[...], first_rest[...]))
+    mixed = dot3(halves(density[...].T), (first_top[...], first_rest[...]))
     real, imag = mixed[:, :512], mixed[:, 512:]
     cos, sin = turn_cos[...], turn_sin[...]
     stacked = jnp.concatenate([real * cos + imag * sin, imag * cos - real * sin], axis=0)
@@ -391,13 +368,7 @@
             jax.ShapeDtypeStruct((NT, TCAP), I32),
             jax.ShapeDtypeStruct((NT, TCAP), I32),
         ),
-        in_specs=[VMEM, VMEM] + [HBM] * len(loaded),
-        scratch_shapes=[pltpu.VMEM(array.shape, array.dtype) for array in loaded]
-        + [
-            pltpu.VMEM((640, 256), BF16),
-            pltpu.VMEM((NT * TH, TW), F32),
-            pltpu.SemaphoreType.DMA((len(loaded),)),
-        ],
+        scratch_shapes=[pltpu.VMEM((640, 256), BF16), pltpu.VMEM((NT * TH, TW), F32)],
         compiler_params=pltpu.CompilerParams(vmem_limit_bytes=40 << 20),
         cost_estimate=pl.CostEstimate(flops=60000000000, bytes_accessed=30000000, transcendentals=0),
         name="spread",
@@ -445,7 +416,9 @@
     out_ref,
 ):
     core = lax.axis_index("c")
-    place = (lax.axis_index("z") * 4 + lax.axis_index("x")) * 4 + lax.axis_index("y")
+    place = 0
+    for name, size in zip(CHIPS, (2, 2, 2, 2, 4, 4)):
+        place = place * size + lax.axis_index(name)
     lane = lax.broadcasted_iota(I32, (128, 512), 1)
     wave_u = lax.broadcasted_iota(I32, (128, 512), 0) + 128 * (lane // 16)
     wave_v = (place // 64) * 16 + lane % 16 + 64 * (place % 64)
@@ -555,12 +528,11 @@
                 ]
         left = jnp.concatenate([part[1] for part in made], axis=1)
         right = jnp.concatenate([part[2] for part in made], axis=1)
-        total[...] += dot_last(left, right)
+        total[...] += dot_last(right, left)
         return carry
 
     lax.fori_loop(0, NT // FORCE_GROUP, step, 0)
-    summed = total[:64, :] + total[64:, :]
-    out_ref[...] = jnp.concatenate([summed, summed], axis=0).T
+    out_ref[...] = total[...] + pltpu.roll(total[...], 64, 1)
 
 
 def tile_forces(got, wide, tall, low, high):
@@ -575,7 +547,7 @@
         ),
         scratch_shapes=[
             pltpu.VMEM((256, 256), F32),
-            pltpu.VMEM((128, 256), F32),
+            pltpu.VMEM((256, 128), F32),
         ],
         compiler_params=pltpu.CompilerParams(vmem_limit_bytes=40 << 20),
         cost_estimate=pl.CostEstimate(flops=40000000000, bytes_accessed=30000000, transcendentals=0),
@@ -606,11 +578,12 @@
         made = [weights(group * GATHER_GROUP + i) for i in range(GATHER_GROUP)]
         left = jnp.concatenate([part[0] for part in made], axis=1)
         right = jnp.concatenate([part[1] for part in made], axis=1)
-        total[...] += dot_last(left, right)
+        total[...] += dot_last(right, left)
         return carry
 
     lax.fori_loop(0, CAP // GATHER_GROUP, step, 0)
-    summed = total[:32, :] + total[32:, :]
+    summed = total[...].T
+    summed = summed[:32] + summed[32:]
     for m in range(2):
         for h in range(16):
             out_ref[m : m + 1, h * LOW : (h + 1) * LOW] = summed[m * 16 + h : m * 16 + h + 1]
@@ -623,7 +596,7 @@
         scratch_shapes=[
             pltpu.VMEM((128, 256), F32),
             pltpu.VMEM((128, 256), F32),
-            pltpu.VMEM((64, 256), F32),
+            pltpu.VMEM((256, 64), F32),
         ],
         compiler_params=pltpu.CompilerParams(vmem_limit_bytes=32 << 20),
         cost_estimate=pl.CostEstimate(flops=20000000000, bytes_accessed=5000000, transcendentals=0),
@@ -634,7 +607,7 @@
 def between_chips(words):
     rows = words.shape[0]
     sent = words.reshape(256, 1, rows // 256 * 128)
-    got = lax.all_to_all(sent, ("z", "x", "y"), split_axis=0, concat_axis=0, tiled=True)
+    got = lax.all_to_all(sent, CHIPS, split_axis=0, concat_axis=0, tiled=True)
     return got.reshape(rows, 128)
 
 
@@ -656,13 +629,12 @@
 
 
 def solution(mesh):
-    fine = Mesh(mesh.devices.reshape(4, 16, 2, 4), ("x", "z", "c", "y"))
-    every = ("x", "z", "c", "y")
-    placed = (P(None, every), P(None, every)) + (P(every, None),) * 5
+    fine = Mesh(mesh.devices.reshape(4, 2, 2, 2, 2, 2, 4), AXES)
+    placed = (P(None, AXES), P(None, AXES)) + (P(AXES, None),) * 5
     return jax.shard_map(
         per_device,
         mesh=fine,
         in_specs=placed,
-        out_specs=(P(None, every, None), P(None, every)),
+        out_specs=(P(None, AXES, None), P(None, AXES)),
         check_vma=False,
     )

time: 164 us -> 160 us (0.976)
  starting transfers between devices: 16.4 us -> 14 us
    ppermute x3, starting transfers between devices: 16.4 us -> 14 us  [with_other(): return (own, lax.ppermute(own, 'c', [(0, 1), (1, 0)]))]
where the time goes in v4:
time: 160 us
  blocking collectives  124 us (78%)
  Pallas kernels  16.7 us (10%)
  starting transfers between devices  14 us (9%)
  waiting for transfers between devices  3.43 us (2%)
    all_to_all x4, blocking collectives, between_chips(): got = lax.all_to_all(sent, CHIPS, split_axis=0, concat_axis=0, tiled=True)  124 us
    ppermute x3, starting transfers between devices, with_other(): return (own, lax.ppermute(own, 'c', [(0, 1), (1, 0)]))  14 us
    pallas_call x1, Pallas kernels, spread(): pl.pallas_call(spread_kernel, out_shape=(jax.ShapeDtypeStruct((256, 128),...  4.78 us
    pallas_call x1, Pallas kernels, tile_forces(): pl.pallas_call(force_kernel, out_shape=(jax.ShapeDtypeStruct((2, TH, GRID...  3.88 us
    pallas_call x1, Pallas kernels, pack_profiles(): pl.pallas_call(pack_kernel, out_shape=(jax.ShapeDtypeStruct((768, 128), I...  3.67 us
    ppermute x3, waiting for transfers between devices, with_other(): return (own, lax.ppermute(own, 'c', [(0, 1), (1, 0)]))  3.43 us
  transfers between devices with their start and end apart: 3, of which 3 were waited for; matrix products, arithmetic and copies ran while one was open for 0% of the time, Pallas kernels for 0%

profile of v4, /device:TPU:1, one launch (start us, length us, event | category | flops | bytes accessed | tf_op | source)
XLA Modules:
  0.0 159.6 jit_solution(11124410884862378303)
XLA Ops:
  0.7 0.0 copy-start.13
  0.7 0.0 copy-start.14
  0.7 0.0 copy-start.15
  0.7 0.0 copy-start.22
  0.7 0.0 copy-start.23
  0.7 3.7 %pack_profiles.1 = (s32[768,128]{1,0:T(8,128)}, s32[16,512]{1,0:T(8,128)}, s32[16,512]{1,0:T(8,128)}) custom-call(bf16[4,4096]{1,0:T(4,128)(2,1)} %row_hbm.1, bf16[16,4096]{1,0:T(8,128)(2,1)} %col_hbm.1, s32[16,512]{1,0:T(8,128)} %bitcast.25), custom_call_target="tpu_custom_call" | custom-call | flops 15000000512 | bytes 10000000 | tf_op jit(solution)/shard_map/pack_profiles/pallas_call | solution.py:232
  4.4 51.2 %all_to_all.20 = s32[256,1,384]{2,1,0:T(1,128)S(1)} all-to-all(s32[256,1,384]{2,1,0:T(1,128)} %bitcast.24), channel_id=1, replica_groups=mesh['x'=4,'z3'=2,'z2'=2,'z1'=2,'z0'=2,'c'=2,'y'=4] {'z0','z1','z2','z3'..., dimensions={0} | all-to-all | bytes 786432 | tf_op jit(solution)/shard_map/all_to_all | solution.py:610
  55.6 0.0 copy-start.18
  55.6 4.0 %collective-permute-start = (s32[768,128]{1,0:T(8,128)S(1)}, s32[768,128]{1,0:T(8,128)S(1)}, u32[]{:S(2)}, u32[]{:S(2)}) collective-permute-start(s32[768,128]{1,0:T(8,128)S(1)} %bitcast.15), channel_id=1, source_target_pairs={{0,4},{4,0},{1,5},{5,1},{2,6},{6,2},{3,7},{7,3},{8,12},{12,8},{9,1... | collective-permute-start | bytes 1179656 | tf_op jit(solution)/shard_map/ppermute | solution.py:615
  59.7 1.3 collective-permute-done.other_ref
  61.1 4.8 %spread.1 = (f32[256,128]{1,0:T(8,128)S(1)}, bf16[4096,256]{1,0:T(8,128)(2,1)S(1)}, f32[256,256]{1,0:T(8,128)S(1)}, s32[32,256]{1,0:T(8,128)S(1)}, s32[32,256]{1,0:T(8,128)S(1)}) custom-call(s32[768,128]{1,0:T(8,128)S(1)} %bitcast.16, s32[768,128]{1,0:T(8,128)S(1)} %collective-permute-done.other_ref, s32[32,256]{1,0:T(8,128)S(1)} %copy-done.1, ...), custom_call_target="tpu_custom_call" | custom-call | flops 60000002048 | bytes 30000000 | tf_op jit(solution)/shard_map/spread/pallas_call | solution.py:362
  65.8 24.6 %all_to_all.21 = f32[256,1,128]{2,1,0:T(1,128)S(1)} all-to-all(f32[256,1,128]{2,1,0:T(1,128)S(1)} %bitcast.19), channel_id=1, replica_groups=mesh['x'=4,'z3'=2,'z2'=2,'z1'=2,'z0'=2,'c'=2,'y'=4] {'z0','z1','z2','z3'..., dimensions={0} | all-to-all | bytes 262144 | tf_op jit(solution)/shard_map/all_to_all | solution.py:610
  90.5 0.0 copy-start.4
  90.5 0.0 copy-start.5
  90.5 0.8 transform_columns.1.own_ref
  91.4 4.7 %collective-permute-start.1 = (f32[128,512]{1,0:T(8,128)S(1)}, f32[128,512]{1,0:T(8,128)S(1)}, u32[]{:S(2)}, u32[]{:S(2)}) collective-permute-start(f32[128,512]{1,0:T(8,128)S(1)} %transform_columns.1.own_ref), channel_id=1, source_target_pairs={{0,4},{4,0},{1,5},{5,1},{2,6},{6,2},{3,7},{7,3},{8,12},{12,8},{9,1... | collective-permute-start | bytes 786440 | tf_op jit(solution)/shard_map/ppermute | solution.py:615
  96.1 1.1 collective-permute-done.1.other_ref
  97.2 1.5 solve_columns.1
  98.7 23.9 %all_to_all.22 = s32[256,1,128]{2,1,0:T(1,128)S(1)} all-to-all(s32[256,1,128]{2,1,0:T(1,128)S(1)} %bitcast.22), channel_id=1, replica_groups=mesh['x'=4,'z3'=2,'z2'=2,'z1'=2,'z0'=2,'c'=2,'y'=4] {'z0','z1','z2','z3'..., dimensions={0} | all-to-all | bytes 262144 | tf_op jit(solution)/shard_map/all_to_all | solution.py:610
  122.7 3.9 %tile_forces.1 = (bf16[2,8,4096]{2,1,0:T(8,128)(2,1)}, f32[256,128]{1,0:T(8,128)S(1)}) custom-call(s32[256,128]{1,0:T(8,128)S(1)} %bitcast.17, bf16[4096,256]{1,0:T(8,128)(2,1)S(1)} %get-tuple-element.14.wide_ref, f32[256,256]{1,0:T(8,128)S(1)} %get-tuple-element.15.tall_ref, s32[32,256]{1,0:T(8,128)S(1)} %get-tuple-element.16.low_ref, ...), custom_call_target="tpu_custom_call" | custom-call | flops 40000000000 | bytes 30000000 | tf_op jit(solution)/shard_map/tile_forces/pallas_call | solution.py:542
  126.6 24.7 %all_to_all.23 = f32[256,1,128]{2,1,0:T(1,128)S(1)} all-to-all(f32[256,1,128]{2,1,0:T(1,128)S(1)} %bitcast.18), channel_id=1, replica_groups=mesh['x'=4,'z3'=2,'z2'=2,'z1'=2,'z0'=2,'c'=2,'y'=4] {'z0','z1','z2','z3'..., dimensions={0} | all-to-all | bytes 262144 | tf_op jit(solution)/shard_map/all_to_all | solution.py:610
  151.3 5.3 %collective-permute-start.2 = (f32[256,128]{1,0:T(8,128)S(1)}, f32[256,128]{1,0:T(8,128)S(1)}, u32[]{:S(2)}, u32[]{:S(2)}) collective-permute-start(f32[256,128]{1,0:T(8,128)S(1)} %bitcast.20), channel_id=1, source_target_pairs={{0,4},{4,0},{1,5},{5,1},{2,6},{6,2},{3,7},{7,3},{8,12},{12,8},{9,1... | collective-permute-start | bytes 393224 | tf_op jit(solution)/shard_map/ppermute | solution.py:615
  156.5 1.0 collective-permute-done.2.other_ref
  157.5 2.1 %gather_forces.1 = f32[2,4096]{1,0:T(2,128)} custom-call(f32[256,128]{1,0:T(8,128)S(1)} %bitcast.21, f32[256,128]{1,0:T(8,128)S(1)} %collective-permute-done.2.other_ref, s32[16,512]{1,0:T(8,128)S(1)} %copy-done.24, s32[16,512]{1,0:T(8,128)S(1)} %copy-done.25), custom_call_target="tpu_custom_call" | custom-call | flops 20000000000 | bytes 5000000 | tf_op jit(solution)/shard_map/gather_forces/pallas_call | solution.py:593
  (44 shorter events, 0.1 us)
Async XLA Ops:
  0.6 60.4 %copy-start = (s32[8,4096]{1,0:T(8,128)S(1)}, s32[8,4096]{1,0:T(8,128)}, u32[]{:S(2)}) copy-start(s32[8,4096]{1,0:T(8,128)} %mask_ref.1) | copy-start | bytes 393220
  0.6 60.3 %copy-start.1 = (s32[32,256]{1,0:T(8,128)S(1)}, s32[32,256]{1,0:T(8,128)}, u32[]{:S(2)}) copy-start(s32[32,256]{1,0:T(8,128)} %list_ref.1) | copy-start | bytes 98308
  0.7 60.3 %copy-start.2 = (s32[32,256]{1,0:T(8,128)S(1)}, s32[32,256]{1,0:T(8,128)}, u32[]{:S(2)}) copy-start(s32[32,256]{1,0:T(8,128)} %row_ref.1) | copy-start | bytes 98308
  0.7 60.3 %copy-start.3 = (s32[32,256]{1,0:T(8,128)S(1)}, s32[32,256]{1,0:T(8,128)}, u32[]{:S(2)}) copy-start(s32[32,256]{1,0:T(8,128)} %col_ref.1) | copy-start | bytes 98308
  0.7 60.3 %copy-start.12 = (bf16[256,1024]{1,0:T(8,128)(2,1)S(1)}, bf16[256,1024]{1,0:T(8,128)(2,1)}, u32[]{:S(2)}) copy-start(bf16[256,1024]{1,0:T(8,128)(2,1)} %constant.41.clone.first_rest) | copy-start | bytes 1572868
  0.7 60.3 %copy-start.13 = (bf16[256,1024]{1,0:T(8,128)(2,1)S(1)}, bf16[256,1024]{1,0:T(8,128)(2,1)}, u32[]{:S(2)}) copy-start(bf16[256,1024]{1,0:T(8,128)(2,1)} %constant.40.clone.first_top) | copy-start | bytes 1572868
  0.7 60.3 %copy-start.14 = (f32[128,512]{1,0:T(8,128)S(1)}, f32[128,512]{1,0:T(8,128)}, u32[]{:S(2)}) copy-start(f32[128,512]{1,0:T(8,128)} %constant.43.clone.turn_sin) | copy-start | bytes 786436
  0.7 60.3 %copy-start.15 = (f32[128,512]{1,0:T(8,128)S(1)}, f32[128,512]{1,0:T(8,128)}, u32[]{:S(2)}) copy-start(f32[128,512]{1,0:T(8,128)} %constant.42.clone.turn_cos) | copy-start | bytes 786436
  0.7 60.3 %copy-start.22 = (bf16[64,256]{1,0:T(8,128)(2,1)S(1)}, bf16[64,256]{1,0:T(8,128)(2,1)}, u32[]{:S(2)}) copy-start(bf16[64,256]{1,0:T(8,128)(2,1)} %constant.45.clone.second_rest) | copy-start | bytes 98308
  0.7 60.3 %copy-start.23 = (bf16[64,256]{1,0:T(8,128)(2,1)S(1)}, bf16[64,256]{1,0:T(8,128)(2,1)}, u32[]{:S(2)}) copy-start(bf16[64,256]{1,0:T(8,128)(2,1)} %constant.44.clone.second_top) | copy-start | bytes 98308
  55.6 34.8 %copy-start.6 = (bf16[1024,512]{1,0:T(8,128)(2,1)S(1)}, bf16[1024,512]{1,0:T(8,128)(2,1)}, u32[]{:S(2)}) copy-start(bf16[1024,512]{1,0:T(8,128)(2,1)} %constant.51.clone.second_rest) | copy-start | bytes 3145732
  55.6 34.8 %copy-start.7 = (bf16[1024,512]{1,0:T(8,128)(2,1)S(1)}, bf16[1024,512]{1,0:T(8,128)(2,1)}, u32[]{:S(2)}) copy-start(bf16[1024,512]{1,0:T(8,128)(2,1)} %constant.50.clone.second_top) | copy-start | bytes 3145732
  55.6 34.8 %copy-start.10 = (f32[8,128,128]{2,1,0:T(8,128)S(1)}, f32[8,128,128]{2,1,0:T(8,128)}, u32[]{:S(2)}) copy-start(f32[8,128,128]{2,1,0:T(8,128)} %constant.49.clone.turn_sin) | copy-start | bytes 1572868
  55.6 34.8 %copy-start.11 = (f32[8,128,128]{2,1,0:T(8,128)S(1)}, f32[8,128,128]{2,1,0:T(8,128)}, u32[]{:S(2)}) copy-start(f32[8,128,128]{2,1,0:T(8,128)} %constant.48.clone.turn_cos) | copy-start | bytes 1572868
  55.6 34.8 %copy-start.18 = (bf16[256,64]{1,0:T(8,128)(2,1)S(1)}, bf16[256,64]{1,0:T(8,128)(2,1)}, u32[]{:S(2)}) copy-start(bf16[256,64]{1,0:T(8,128)(2,1)} %constant.47.clone.first_rest) | copy-start | bytes 98308
  55.6 34.8 %copy-start.19 = (bf16[256,64]{1,0:T(8,128)(2,1)S(1)}, bf16[256,64]{1,0:T(8,128)(2,1)}, u32[]{:S(2)}) copy-start(bf16[256,64]{1,0:T(8,128)(2,1)} %constant.46.clone.first_top) | copy-start | bytes 98308
  55.6 5.4 %collective-permute-start = (s32[768,128]{1,0:T(8,128)S(1)}, s32[768,128]{1,0:T(8,128)S(1)}, u32[]{:S(2)}, u32[]{:S(2)}) collective-permute-start(s32[768,128]{1,0:T(8,128)S(1)} %bitcast.15), channel_id=1, source_target_pairs={{0,4},{4,0},{1,5},{5,1},{2,6},{6,2},{3,7},{7,3},{8,12},{12,8},{9,1... | collective-permute-start | bytes 1179656 | tf_op jit(solution)/shard_map/ppermute | solution.py:615
  91.3 31.3 %copy-start.8 = (bf16[1024,256]{1,0:T(8,128)(2,1)S(1)}, bf16[1024,256]{1,0:T(8,128)(2,1)}, u32[]{:S(2)}) copy-start(bf16[1024,256]{1,0:T(8,128)(2,1)} %constant.59.clone.last_rest) | copy-start | bytes 1572868
  91.4 31.3 %copy-start.9 = (bf16[1024,256]{1,0:T(8,128)(2,1)S(1)}, bf16[1024,256]{1,0:T(8,128)(2,1)}, u32[]{:S(2)}) copy-start(bf16[1024,256]{1,0:T(8,128)(2,1)} %constant.58.clone.last_top) | copy-start | bytes 1572868
  91.4 31.3 %copy-start.16 = (bf16[256,64]{1,0:T(8,128)(2,1)S(1)}, bf16[256,64]{1,0:T(8,128)(2,1)}, u32[]{:S(2)}) copy-start(bf16[256,64]{1,0:T(8,128)(2,1)} %constant.57.clone.wave_rest) | copy-start | bytes 98308
  91.4 5.8 %collective-permute-start.1 = (f32[128,512]{1,0:T(8,128)S(1)}, f32[128,512]{1,0:T(8,128)S(1)}, u32[]{:S(2)}, u32[]{:S(2)}) collective-permute-start(f32[128,512]{1,0:T(8,128)S(1)} %transform_columns.1.own_ref), channel_id=1, source_target_pairs={{0,4},{4,0},{1,5},{5,1},{2,6},{6,2},{3,7},{7,3},{8,12},{12,8},{9,1... | collective-permute-start | bytes 786440 | tf_op jit(solution)/shard_map/ppermute | solution.py:615
  122.7 34.8 %copy-start.24 = (s32[16,512]{1,0:T(8,128)S(1)}, s32[16,512]{1,0:T(8,128)}, u32[]{:S(2)}) copy-start(s32[16,512]{1,0:T(8,128)} %get-tuple-element.20.low_ref) | copy-start | bytes 98308
  122.7 34.8 %copy-start.25 = (s32[16,512]{1,0:T(8,128)S(1)}, s32[16,512]{1,0:T(8,128)}, u32[]{:S(2)}) copy-start(s32[16,512]{1,0:T(8,128)} %get-tuple-element.21.high_ref) | copy-start | bytes 98308
  151.3 6.2 %collective-permute-start.2 = (f32[256,128]{1,0:T(8,128)S(1)}, f32[256,128]{1,0:T(8,128)S(1)}, u32[]{:S(2)}, u32[]{:S(2)}) collective-permute-start(f32[256,128]{1,0:T(8,128)S(1)} %bitcast.20), channel_id=1, source_target_pairs={{0,4},{4,0},{1,5},{5,1},{2,6},{6,2},{3,7},{7,3},{8,12},{12,8},{9,1... | collective-permute-start | bytes 393224 | tf_op jit(solution)/shard_map/ppermute | solution.py:615
  (5 other events, 58.4 us)

commit v5 on v4

--- a/solution.py
+++ b/solution.py
@@ -26,7 +26,6 @@
 STEPS = 819.0
 SPREAD_GROUP = 32
 FORCE_GROUP = 16
-GATHER_GROUP = 16
 F32 = jnp.float32
 BF16 = jnp.bfloat16
 I32 = jnp.int32
@@ -260,10 +259,49 @@
     return low, high
 
 
+def unpack(words):
+    return [
+        (piece.astype(F32) * (1.0 / SCALE)).astype(BF16) for piece in (words & 0xFFFF, words >> 16)
+    ]
+
+
+def unpack_side(side, ref):
+    cols = unpack(ref[pl.ds(side, 256, stride=3), :].T)
+    rows = ref[pl.ds(2, 256, stride=3), :].T
+    return cols, unpack(rows[side * 32 : side * 32 + 32])
+
+
+def own_half_kernel(own_ref, list_ref, table_ref, low_ref, high_ref):
+    low, high = slot_address(list_ref[...], lax.axis_index("c"))
+    low_ref[...] = low
+    high_ref[...] = high
+    cols, rows = unpack_side(0, own_ref)
+    for part in range(2):
+        table_ref[part * 128 : part * 128 + 128, :] = cols[part]
+        table_ref[256 + part * 32 : 288 + part * 32, :] = rows[part]
+
+
+def own_half(own, tile_list):
+    return pl.pallas_call(
+        own_half_kernel,
+        out_shape=(
+            jax.ShapeDtypeStruct((320, 256), BF16),
+            jax.ShapeDtypeStruct((NT, TCAP), I32),
+            jax.ShapeDtypeStruct((NT, TCAP), I32),
+        ),
+        compiler_params=pltpu.CompilerParams(vmem_limit_bytes=32 << 20),
+        cost_estimate=pl.CostEstimate(
+            flops=5000000000, bytes_accessed=2500000, transcendentals=0
+        ),
+        name="own_half",
+    )(own, tile_list)
+
+
 def spread_kernel(
-    own_ref,
+    half_ref,
     other_ref,
-    list_ref,
+    low_ref,
+    high_ref,
     row_ref,
     col_ref,
     mask_ref,
@@ -276,26 +314,16 @@
     out_ref,
     wide_ref,
     tall_ref,
-    low_ref,
-    high_ref,
     table,
     density,
 ):
-    core = lax.axis_index("c")
-    for s, ref in enumerate((own_ref, other_ref)):
-        words = ref[pl.ds(s, 256, stride=3), :].T
-        for part, piece in enumerate((words & 0xFFFF, words >> 16)):
-            start = s * 256 + part * 128
-            table[start : start + 128, :] = (piece.astype(F32) * (1.0 / SCALE)).astype(BF16)
-    own_rows = own_ref[pl.ds(2, 256, stride=3), :].T
-    other_rows = other_ref[pl.ds(2, 256, stride=3), :].T
-    words = jnp.concatenate([own_rows[:32], other_rows[32:64]], axis=0)
-    for part, piece in enumerate((words & 0xFFFF, words >> 16)):
+    cols, rows = unpack_side(1, other_ref)
+    table[0:256, :] = half_ref[0:256, :]
+    for part in range(2):
         start = 512 + part * 64
-        table[start : start + 64, :] = (piece.astype(F32) * (1.0 / SCALE)).astype(BF16)
-    low, high = slot_address(list_ref[...], core)
-    low_ref[...] = low
-    high_ref[...] = high
+        table[256 + part * 128 : 384 + part * 128, :] = cols[part]
+        table[start : start + 32, :] = half_ref[256 + part * 32 : 288 + part * 32, :]
+        table[start + 32 : start + 64, :] = rows[part]
     upper = lax.broadcasted_iota(I32, (8, TCAP), 0) // 4
     zero = jnp.zeros((8, TCAP), F32)
 
@@ -356,23 +384,21 @@
         out_ref[q * 64 : q * 64 + 64, :] = result[:, q * 128 : q * 128 + 128]
 
 
-def spread(own, other, tile_list, row_offset, col_offset, macro_mask):
+def spread(half, other, low, high, row_offset, col_offset, macro_mask):
     first, cos, sin, second = tables_x()
-    loaded = (tile_list, row_offset, col_offset, macro_mask, *first, cos, sin, *second)
+    loaded = (row_offset, col_offset, macro_mask, *first, cos, sin, *second)
     return pl.pallas_call(
         spread_kernel,
         out_shape=(
             jax.ShapeDtypeStruct((256, 128), F32),
             jax.ShapeDtypeStruct((NT * TW, TCAP), BF16),
             jax.ShapeDtypeStruct((NT * TH, TCAP), F32),
-            jax.ShapeDtypeStruct((NT, TCAP), I32),
-            jax.ShapeDtypeStruct((NT, TCAP), I32),
         ),
         scratch_shapes=[pltpu.VMEM((640, 256), BF16), pltpu.VMEM((NT * TH, TW), F32)],
         compiler_params=pltpu.CompilerParams(vmem_limit_bytes=40 << 20),
         cost_estimate=pl.CostEstimate(flops=60000000000, bytes_accessed=30000000, transcendentals=0),
         name="spread",
-    )(own, other, *loaded)
+    )(half, other, low, high, *loaded)
 
 
 def column_kernel(
@@ -555,53 +581,53 @@
     )(got, wide, tall, low, high, *wave, cos, sin, *last)
 
 
-def gather_kernel(own_ref, other_ref, low_ref, high_ref, out_ref, own, other, total):
-    own[...] = own_ref[...].T
-    other[...] = other_ref[...].T
-    total[...] = jnp.zeros_like(total)
-    lines = lax.broadcasted_iota(I32, (16, 512), 0)
-
-    def weights(k):
-        chosen = lines == high_ref[pl.ds(k, 1), :]
+def gather_part(side, got_ref, low_ref, high_ref, got):
+    got[...] = got_ref[...].T
+    lines = lax.broadcasted_iota(I32, (16, 256), 0)
+    here = slice(side * 256, side * 256 + 256)
+    lefts, rights = [], []
+    for k in range(CAP):
+        chosen = lines == high_ref[k : k + 1, here]
         tops, rests = [], []
         for m in range(2):
-            force = jnp.concatenate(
-                [own[pl.ds(m * 32 + k, 1), :], other[pl.ds(m * 32 + 16 + k, 1), :]], axis=1
-            )
+            row = m * 32 + side * 16 + k
+            force = got[row : row + 1, :]
             top = force.astype(BF16).astype(F32)
             tops.append(jnp.where(chosen, top, 0.0))
             rests.append(jnp.where(chosen, force - top, 0.0))
-        left = jnp.concatenate(tops + rests, axis=0).astype(BF16)
-        return left, one_hot(low_ref[pl.ds(k, 1), :], LOW)
-
-    def step(group, carry):
-        made = [weights(group * GATHER_GROUP + i) for i in range(GATHER_GROUP)]
-        left = jnp.concatenate([part[0] for part in made], axis=1)
-        right = jnp.concatenate([part[1] for part in made], axis=1)
-        total[...] += dot_last(right, left)
-        return carry
-
-    lax.fori_loop(0, CAP // GATHER_GROUP, step, 0)
-    summed = total[...].T
+        lefts.append(jnp.concatenate(tops + rests, axis=0).astype(BF16))
+        rights.append(one_hot(low_ref[k : k + 1, here], LOW))
+    return dot_last(jnp.concatenate(rights, axis=1), jnp.concatenate(lefts, axis=1))
+
+
+def gather_own_kernel(got_ref, low_ref, high_ref, out_ref, got):
+    out_ref[...] = gather_part(0, got_ref, low_ref, high_ref, got)
+
+
+def gather_kernel(own_ref, got_ref, low_ref, high_ref, out_ref, got):
+    summed = (own_ref[...] + gather_part(1, got_ref, low_ref, high_ref, got)).T
     summed = summed[:32] + summed[32:]
     for m in range(2):
         for h in range(16):
             out_ref[m : m + 1, h * LOW : (h + 1) * LOW] = summed[m * 16 + h : m * 16 + h + 1]
 
 
+def gather_call(kernel, shape, name):
+    return pl.pallas_call(
+        kernel,
+        out_shape=jax.ShapeDtypeStruct(shape, F32),
+        scratch_shapes=[pltpu.VMEM((128, 256), F32)],
+        compiler_params=pltpu.CompilerParams(vmem_limit_bytes=32 << 20),
+        cost_estimate=pl.CostEstimate(
+            flops=10000000000, bytes_accessed=2500000, transcendentals=0
+        ),
+        name=name,
+    )
+
+
 def gather_forces(own, other, low, high):
-    return pl.pallas_call(
-        gather_kernel,
-        out_shape=jax.ShapeDtypeStruct((2, CELL_DEV), F32),
-        scratch_shapes=[
-            pltpu.VMEM((128, 256), F32),
-            pltpu.VMEM((128, 256), F32),
-            pltpu.VMEM((256, 64), F32),
-        ],
-        compiler_params=pltpu.CompilerParams(vmem_limit_bytes=32 << 20),
-        cost_estimate=pl.CostEstimate(flops=20000000000, bytes_accessed=5000000, transcendentals=0),
-        name="gather_forces",
-    )(own, other, low, high)
+    part = gather_call(gather_own_kernel, (256, 64), "gather_own")(own, low, high)
+    return gather_call(gather_kernel, (2, CELL_DEV), "gather_forces")(part, other, low, high)
 
 
 def between_chips(words):
@@ -618,8 +644,9 @@
 def per_device(row_profile, col_profile, send_list, tile_list, row_offset, col_offset, macro_mask):
     words, cell_low, cell_high = pack_profiles(row_profile, col_profile, send_list)
     own, other = with_other(between_chips(words))
-    lines, wide, tall, slot_low, slot_high = spread(
-        own, other, tile_list, row_offset, col_offset, macro_mask
+    half, slot_low, slot_high = own_half(own, tile_list)
+    lines, wide, tall = spread(
+        half, other, slot_low, slot_high, row_offset, col_offset, macro_mask
     )
     partial = transform_columns(between_chips(lines))
     maps = solve_columns(*with_other(partial))

time: 160 us -> 159 us (level)
  transfers between devices with their start and end apart: 3 -> 3, of which waited for: 3 -> 3; matrix products, arithmetic and copies ran while one was open for 0% -> 0% of each run, Pallas kernels for 0% -> 1%
where the time goes in v5:
time: 159 us
  blocking collectives  124 us (78%)
  Pallas kernels  16.8 us (11%)
  starting transfers between devices  13.9 us (9%)
  waiting for transfers between devices  2.4 us (2%)
    all_to_all x4, blocking collectives, between_chips(): got = lax.all_to_all(sent, CHIPS, split_axis=0, concat_axis=0, tiled=True)  124 us
    ppermute x3, starting transfers between devices, with_other(): return (own, lax.ppermute(own, 'c', [(0, 1), (1, 0)]))  13.9 us
    pallas_call x1, Pallas kernels, spread(): pl.pallas_call(spread_kernel, out_shape=(jax.ShapeDtypeStruct((256, 128),...  4.66 us
    pallas_call x1, Pallas kernels, tile_forces(): pl.pallas_call(force_kernel, out_shape=(jax.ShapeDtypeStruct((2, TH, GRID...  3.87 us
    pallas_call x1, Pallas kernels, pack_profiles(): pl.pallas_call(pack_kernel, out_shape=(jax.ShapeDtypeStruct((768, 128), I...  3.55 us
  transfers between devices with their start and end apart: 3, of which 3 were waited for; matrix products, arithmetic and copies ran while one was open for 0% of the time, Pallas kernels for 1%

profile of v5, /device:TPU:1, one launch (start us, length us, event | category | flops | bytes accessed | tf_op | source)
XLA Modules:
  0.0 158.6 jit_solution(7648866880083491077)
XLA Ops:
  0.6 3.5 %pack_profiles.1 = (s32[768,128]{1,0:T(8,128)}, s32[16,512]{1,0:T(8,128)}, s32[16,512]{1,0:T(8,128)}) custom-call(bf16[4,4096]{1,0:T(4,128)(2,1)} %row_hbm.1, bf16[16,4096]{1,0:T(8,128)(2,1)} %col_hbm.1, s32[16,512]{1,0:T(8,128)} %bitcast.25), custom_call_target="tpu_custom_call" | custom-call | flops 15000000512 | bytes 10000000 | tf_op jit(solution)/shard_map/pack_profiles/pallas_call | solution.py:231
  4.2 51.2 %all_to_all.20 = s32[256,1,384]{2,1,0:T(1,128)S(1)} all-to-all(s32[256,1,384]{2,1,0:T(1,128)} %bitcast.24), channel_id=1, replica_groups=mesh['x'=4,'z3'=2,'z2'=2,'z1'=2,'z0'=2,'c'=2,'y'=4] {'z0','z1','z2','z3'..., dimensions={0} | all-to-all | bytes 786432 | tf_op jit(solution)/shard_map/all_to_all | solution.py:636
  55.4 0.0 copy-start.13
  55.4 0.0 copy-start.15
  55.4 0.0 copy-start.22
  55.4 0.0 copy-start.23
  55.4 3.9 %collective-permute-start = (s32[768,128]{1,0:T(8,128)S(1)}, s32[768,128]{1,0:T(8,128)S(1)}, u32[]{:S(2)}, u32[]{:S(2)}) collective-permute-start(s32[768,128]{1,0:T(8,128)S(1)} %bitcast.15), channel_id=1, source_target_pairs={{0,4},{4,0},{1,5},{5,1},{2,6},{6,2},{3,7},{7,3},{8,12},{12,8},{9,1... | collective-permute-start | bytes 1179656 | tf_op jit(solution)/shard_map/ppermute | solution.py:641
  59.4 0.2 own_half.1
  59.6 1.1 collective-permute-done.other_ref
  60.7 0.0 copy-start.6
  60.7 0.0 copy-start.7
  60.8 4.7 %spread.1 = (f32[256,128]{1,0:T(8,128)S(1)}, bf16[4096,256]{1,0:T(8,128)(2,1)S(1)}, f32[256,256]{1,0:T(8,128)S(1)}) custom-call(bf16[320,256]{1,0:T(8,128)(2,1)S(1)} %get-tuple-element.14.half_ref, s32[768,128]{1,0:T(8,128)S(1)} %collective-permute-done.other_ref, s32[32,256]{1,0:T(8,128)S(1)} %get-tuple-element.15.low_ref, ...), custom_call_target="tpu_custom_call" | custom-call | flops 60000002048 | bytes 30000000 | tf_op jit(solution)/shard_map/spread/pallas_call | solution.py:390
  65.5 24.6 %all_to_all.21 = f32[256,1,128]{2,1,0:T(1,128)S(1)} all-to-all(f32[256,1,128]{2,1,0:T(1,128)S(1)} %bitcast.19), channel_id=1, replica_groups=mesh['x'=4,'z3'=2,'z2'=2,'z1'=2,'z0'=2,'c'=2,'y'=4] {'z0','z1','z2','z3'..., dimensions={0} | all-to-all | bytes 262144 | tf_op jit(solution)/shard_map/all_to_all | solution.py:636
  90.1 0.8 transform_columns.1.own_ref
  91.0 4.7 %collective-permute-start.1 = (f32[128,512]{1,0:T(8,128)S(1)}, f32[128,512]{1,0:T(8,128)S(1)}, u32[]{:S(2)}, u32[]{:S(2)}) collective-permute-start(f32[128,512]{1,0:T(8,128)S(1)} %transform_columns.1.own_ref), channel_id=1, source_target_pairs={{0,4},{4,0},{1,5},{5,1},{2,6},{6,2},{3,7},{7,3},{8,12},{12,8},{9,1... | collective-permute-start | bytes 786440 | tf_op jit(solution)/shard_map/ppermute | solution.py:641
  95.7 1.1 collective-permute-done.1.other_ref
  96.9 1.5 solve_columns.1
  98.4 23.9 %all_to_all.22 = s32[256,1,128]{2,1,0:T(1,128)S(1)} all-to-all(s32[256,1,128]{2,1,0:T(1,128)S(1)} %bitcast.20), channel_id=1, replica_groups=mesh['x'=4,'z3'=2,'z2'=2,'z1'=2,'z0'=2,'c'=2,'y'=4] {'z0','z1','z2','z3'..., dimensions={0} | all-to-all | bytes 262144 | tf_op jit(solution)/shard_map/all_to_all | solution.py:636
  122.3 3.9 %tile_forces.1 = (bf16[2,8,4096]{2,1,0:T(8,128)(2,1)}, f32[256,128]{1,0:T(8,128)S(1)}) custom-call(s32[256,128]{1,0:T(8,128)S(1)} %bitcast.17, bf16[4096,256]{1,0:T(8,128)(2,1)S(1)} %get-tuple-element.18.wide_ref, f32[256,256]{1,0:T(8,128)S(1)} %get-tuple-element.19.tall_ref, s32[32,256]{1,0:T(8,128)S(1)} %get-tuple-element.15.low_ref, ...), custom_call_target="tpu_custom_call" | custom-call | flops 40000000000 | bytes 30000000 | tf_op jit(solution)/shard_map/tile_forces/pallas_call | solution.py:568
  126.2 24.7 %all_to_all.23 = f32[256,1,128]{2,1,0:T(1,128)S(1)} all-to-all(f32[256,1,128]{2,1,0:T(1,128)S(1)} %bitcast.18), channel_id=1, replica_groups=mesh['x'=4,'z3'=2,'z2'=2,'z1'=2,'z0'=2,'c'=2,'y'=4] {'z0','z1','z2','z3'..., dimensions={0} | all-to-all | bytes 262144 | tf_op jit(solution)/shard_map/all_to_all | solution.py:636
  150.9 5.3 %collective-permute-start.2 = (f32[256,128]{1,0:T(8,128)S(1)}, f32[256,128]{1,0:T(8,128)S(1)}, u32[]{:S(2)}, u32[]{:S(2)}) collective-permute-start(f32[256,128]{1,0:T(8,128)S(1)} %bitcast.21), channel_id=1, source_target_pairs={{0,4},{4,0},{1,5},{5,1},{2,6},{6,2},{3,7},{7,3},{8,12},{12,8},{9,1... | collective-permute-start | bytes 393224 | tf_op jit(solution)/shard_map/ppermute | solution.py:641
  156.2 0.8 gather_own.1.own_ref
  156.9 0.2 collective-permute-done.2.got_ref
  157.1 1.5 gather_forces.1
  (46 shorter events, 0.1 us)
Async XLA Ops:
  0.6 58.7 %copy-start.1 = (s32[32,256]{1,0:T(8,128)S(1)}, s32[32,256]{1,0:T(8,128)}, u32[]{:S(2)}) copy-start(s32[32,256]{1,0:T(8,128)} %list_ref.1) | copy-start | bytes 98308
  55.4 5.3 %copy-start.2 = (s32[32,256]{1,0:T(8,128)S(1)}, s32[32,256]{1,0:T(8,128)}, u32[]{:S(2)}) copy-start(s32[32,256]{1,0:T(8,128)} %row_ref.1) | copy-start | bytes 98308
  55.4 5.3 %copy-start.3 = (s32[32,256]{1,0:T(8,128)S(1)}, s32[32,256]{1,0:T(8,128)}, u32[]{:S(2)}) copy-start(s32[32,256]{1,0:T(8,128)} %col_ref.1) | copy-start | bytes 98308
  55.4 5.3 %copy-start.12 = (bf16[256,1024]{1,0:T(8,128)(2,1)S(1)}, bf16[256,1024]{1,0:T(8,128)(2,1)}, u32[]{:S(2)}) copy-start(bf16[256,1024]{1,0:T(8,128)(2,1)} %constant.41.clone.first_rest) | copy-start | bytes 1572868
  55.4 5.3 %copy-start.13 = (bf16[256,1024]{1,0:T(8,128)(2,1)S(1)}, bf16[256,1024]{1,0:T(8,128)(2,1)}, u32[]{:S(2)}) copy-start(bf16[256,1024]{1,0:T(8,128)(2,1)} %constant.40.clone.first_top) | copy-start | bytes 1572868
  55.4 5.2 %collective-permute-start = (s32[768,128]{1,0:T(8,128)S(1)}, s32[768,128]{1,0:T(8,128)S(1)}, u32[]{:S(2)}, u32[]{:S(2)}) collective-permute-start(s32[768,128]{1,0:T(8,128)S(1)} %bitcast.15), channel_id=1, source_target_pairs={{0,4},{4,0},{1,5},{5,1},{2,6},{6,2},{3,7},{7,3},{8,12},{12,8},{9,1... | collective-permute-start | bytes 1179656 | tf_op jit(solution)/shard_map/ppermute | solution.py:641
  60.7 29.3 %copy-start.6 = (bf16[1024,512]{1,0:T(8,128)(2,1)S(1)}, bf16[1024,512]{1,0:T(8,128)(2,1)}, u32[]{:S(2)}) copy-start(bf16[1024,512]{1,0:T(8,128)(2,1)} %constant.51.clone.second_rest) | copy-start | bytes 3145732
  60.7 29.3 %copy-start.7 = (bf16[1024,512]{1,0:T(8,128)(2,1)S(1)}, bf16[1024,512]{1,0:T(8,128)(2,1)}, u32[]{:S(2)}) copy-start(bf16[1024,512]{1,0:T(8,128)(2,1)} %constant.50.clone.second_top) | copy-start | bytes 3145732
  60.8 29.3 %copy-start.10 = (f32[8,128,128]{2,1,0:T(8,128)S(1)}, f32[8,128,128]{2,1,0:T(8,128)}, u32[]{:S(2)}) copy-start(f32[8,128,128]{2,1,0:T(8,128)} %constant.49.clone.turn_sin) | copy-start | bytes 1572868
  60.8 29.3 %copy-start.11 = (f32[8,128,128]{2,1,0:T(8,128)S(1)}, f32[8,128,128]{2,1,0:T(8,128)}, u32[]{:S(2)}) copy-start(f32[8,128,128]{2,1,0:T(8,128)} %constant.48.clone.turn_cos) | copy-start | bytes 1572868
  60.8 29.3 %copy-start.18 = (bf16[256,64]{1,0:T(8,128)(2,1)S(1)}, bf16[256,64]{1,0:T(8,128)(2,1)}, u32[]{:S(2)}) copy-start(bf16[256,64]{1,0:T(8,128)(2,1)} %constant.47.clone.first_rest) | copy-start | bytes 98308
  60.8 29.3 %copy-start.19 = (bf16[256,64]{1,0:T(8,128)(2,1)S(1)}, bf16[256,64]{1,0:T(8,128)(2,1)}, u32[]{:S(2)}) copy-start(bf16[256,64]{1,0:T(8,128)(2,1)} %constant.46.clone.first_top) | copy-start | bytes 98308
  90.1 6.8 %copy-start.4 = (bf16[512,1024]{1,0:T(8,128)(2,1)S(1)}, bf16[512,1024]{1,0:T(8,128)(2,1)}, u32[]{:S(2)}) copy-start(bf16[512,1024]{1,0:T(8,128)(2,1)} %constant.55.clone.wave_rest) | copy-start | bytes 3145732
  90.1 6.8 %copy-start.5 = (bf16[512,1024]{1,0:T(8,128)(2,1)S(1)}, bf16[512,1024]{1,0:T(8,128)(2,1)}, u32[]{:S(2)}) copy-start(bf16[512,1024]{1,0:T(8,128)(2,1)} %constant.54.clone.wave_top) | copy-start | bytes 3145732
  90.1 6.8 %copy-start.20 = (bf16[64,256]{1,0:T(8,128)(2,1)S(1)}, bf16[64,256]{1,0:T(8,128)(2,1)}, u32[]{:S(2)}) copy-start(bf16[64,256]{1,0:T(8,128)(2,1)} %constant.53.clone.back_rest) | copy-start | bytes 98308
  90.1 6.8 %copy-start.21 = (bf16[64,256]{1,0:T(8,128)(2,1)S(1)}, bf16[64,256]{1,0:T(8,128)(2,1)}, u32[]{:S(2)}) copy-start(bf16[64,256]{1,0:T(8,128)(2,1)} %constant.52.clone.back_top) | copy-start | bytes 98308
  90.9 31.4 %copy-start.8 = (bf16[1024,256]{1,0:T(8,128)(2,1)S(1)}, bf16[1024,256]{1,0:T(8,128)(2,1)}, u32[]{:S(2)}) copy-start(bf16[1024,256]{1,0:T(8,128)(2,1)} %constant.59.clone.last_rest) | copy-start | bytes 1572868
  91.0 31.3 %copy-start.9 = (bf16[1024,256]{1,0:T(8,128)(2,1)S(1)}, bf16[1024,256]{1,0:T(8,128)(2,1)}, u32[]{:S(2)}) copy-start(bf16[1024,256]{1,0:T(8,128)(2,1)} %constant.58.clone.last_top) | copy-start | bytes 1572868
  91.0 31.3 %copy-start.16 = (bf16[256,64]{1,0:T(8,128)(2,1)S(1)}, bf16[256,64]{1,0:T(8,128)(2,1)}, u32[]{:S(2)}) copy-start(bf16[256,64]{1,0:T(8,128)(2,1)} %constant.57.clone.wave_rest) | copy-start | bytes 98308
  91.0 31.3 %copy-start.17 = (bf16[256,64]{1,0:T(8,128)(2,1)S(1)}, bf16[256,64]{1,0:T(8,128)(2,1)}, u32[]{:S(2)}) copy-start(bf16[256,64]{1,0:T(8,128)(2,1)} %constant.56.clone.wave_top) | copy-start | bytes 98308
  91.0 5.9 %collective-permute-start.1 = (f32[128,512]{1,0:T(8,128)S(1)}, f32[128,512]{1,0:T(8,128)S(1)}, u32[]{:S(2)}, u32[]{:S(2)}) collective-permute-start(f32[128,512]{1,0:T(8,128)S(1)} %transform_columns.1.own_ref), channel_id=1, source_target_pairs={{0,4},{4,0},{1,5},{5,1},{2,6},{6,2},{3,7},{7,3},{8,12},{12,8},{9,1... | collective-permute-start | bytes 786440 | tf_op jit(solution)/shard_map/ppermute | solution.py:641
  122.3 33.8 %copy-start.24 = (s32[16,512]{1,0:T(8,128)S(1)}, s32[16,512]{1,0:T(8,128)}, u32[]{:S(2)}) copy-start(s32[16,512]{1,0:T(8,128)} %get-tuple-element.22.low_ref) | copy-start | bytes 98308
  122.3 33.8 %copy-start.25 = (s32[16,512]{1,0:T(8,128)S(1)}, s32[16,512]{1,0:T(8,128)}, u32[]{:S(2)}) copy-start(s32[16,512]{1,0:T(8,128)} %get-tuple-element.23.high_ref) | copy-start | bytes 98308
  150.9 6.2 %collective-permute-start.2 = (f32[256,128]{1,0:T(8,128)S(1)}, f32[256,128]{1,0:T(8,128)S(1)}, u32[]{:S(2)}, u32[]{:S(2)}) collective-permute-start(f32[256,128]{1,0:T(8,128)S(1)} %bitcast.21), channel_id=1, source_target_pairs={{0,4},{4,0},{1,5},{5,1},{2,6},{6,2},{3,7},{7,3},{8,12},{12,8},{9,1... | collective-permute-start | bytes 393224 | tf_op jit(solution)/shard_map/ppermute | solution.py:641
  (5 other events, 26.5 us)
